TPU v7x, 256 devices: a whole 4x4x8 slice. The times are simulated.
256 devices in a mesh: dp: 32 (over z, x), head: 8 (over y, core).
Axes of the slice: x: 4, y: 4, z: 8, core: 2. Of those that a mesh axis runs over, the one named last changes fastest.
Arguments:
- tokens: bfloat16 [32768, 2048], P(('dp', 'head')), may hold values from -8 to 8
- stretch_prompt: int32 [64], replicated, may hold values from 0 to 7, never falling along the last dimension, each value on 1 to 32 neighbouring positions
- last_fill: int32 [64], replicated, may hold values from 1 to 512
- ln1_gain: bfloat16 [2048], replicated, may hold values from 0.25 to 1.75
- w_qk: bfloat16 [2048, 2, 2048], P(None, None, 'head'), may hold values from -0.125 to 0.125
- w_vz: bfloat16 [2048, 2, 4096], P(None, None, 'head'), may hold values from -0.125 to 0.125
- w_ba: bfloat16 [2048, 2, 32], P(None, None, 'head'), may hold values from -2 to 2
- conv_qk: bfloat16 [4, 2, 2048], P(None, None, 'head'), may hold values from -3 to 3
- conv_value: bfloat16 [4, 4096], P(None, 'head'), may hold values from -3 to 3
- decay_log: float32 [32], P('head'), may hold values from 0 to 1
- dt_bias: float32 [32], P('head'), may hold values from -25 to -3
- norm_gain: bfloat16 [128], replicated, may hold values from 0.25 to 1.75
- w_out: bfloat16 [4096, 2048], P('head'), may hold values from -0.09375 to 0.09375
- ln2_gain: bfloat16 [2048], replicated, may hold values from 0.25 to 1.75
- w_sgate: bfloat16 [2048], replicated, may hold values from -0.125 to 0.125
- shared_weights: bfloat16 [3, 512, 2048], P(None, 'head'), may hold values from -0.25 to 0.25
Outputs:
- attention_out: bfloat16 [32768, 2048], P(('dp', 'head'))
- layer_out: bfloat16 [32768, 2048], P(('dp', 'head'))
Inputs may be any that keep to these rules, and one draw needn't show every extreme that they name: stretch_prompt never falls from one stretch to the next, so each prompt holds consecutive stretches; every prompt holds 1 to 32 stretches and one holds exactly 32.
All inputs are finite; a program needn't handle non-finite values.
Results may differ from a plain program's by a relative error of at most 0.025.
Values may be sent and summed in bfloat16 or wider, within the bound.
No kernel may reach another device: no remote copies, remote signals or barrier semaphores. Data moves between devices by JAX's collectives and lax.ppermute only.
A program may use at most 128 MiB of HBM per device.

v0:
```python
import jax
import jax.numpy as jnp
from jax import lax
from jax.sharding import PartitionSpec as P

DK = 128
DV = 128
BLOCK = 64
STRETCH = 512
SLOTS = 2


HIGHEST = lax.Precision.HIGHEST
EPSILON = 1e-06


def shifted(value, axis, steps):
    count = lax.axis_size(axis)
    first, last = (max(0, -steps), min(count, count - steps))
    return lax.ppermute(value, axis, [(source, source + steps) for source in range(first, last)])


def matmul_high(left, right):
    return jnp.einsum("...ij,...jk->...ik", left, right, precision=HIGHEST)


def scaled_rows(inputs, scaling):
    widened = inputs.astype(jnp.float32)
    spread = jnp.mean(widened * widened, axis=-1, keepdims=True)
    return widened * lax.rsqrt(spread + EPSILON) * scaling.astype(jnp.float32)


def unit_rows(inputs):
    return inputs * lax.rsqrt(jnp.sum(inputs * inputs, axis=-1, keepdims=True) + EPSILON)


def inverse_unit_lower(strict_part):
    span = strict_part.shape[-1]
    identity_block = jnp.eye(span, dtype=jnp.float32)
    negated = -strict_part
    inverse = identity_block + negated
    powered = negated
    for doubling in range(1, (span - 1).bit_length()):
        powered = matmul_high(powered, powered)
        inverse = matmul_high(inverse, identity_block + powered)
    return inverse


def block_terms(query, keys, values, beta, rate):
    span = query.shape[-2]
    positions = jnp.arange(span)
    inclusive = positions[:, None] >= positions[None, :]
    strict = positions[:, None] > positions[None, :]
    summing = inclusive.astype(jnp.float32)
    log_decay = jnp.einsum("...j,ij->...i", rate, summing, precision=HIGHEST)
    spread = log_decay[..., :, None] - log_decay[..., None, :]
    weight_in = jnp.where(inclusive, jnp.exp(jnp.where(inclusive, spread, 0.0)), 0.0)
    weight_strict = jnp.where(strict, weight_in, 0.0)
    scaled_keys = keys * beta[..., None]
    mixing = jnp.einsum("...id,...jd->...ij", scaled_keys, keys, precision=HIGHEST) * weight_strict
    scores = jnp.einsum("...id,...jd->...ij", query, keys, precision=HIGHEST) * weight_in
    growth = jnp.exp(log_decay)
    inverse = inverse_unit_lower(mixing)
    w_rows = matmul_high(inverse, scaled_keys * growth[..., None])
    u_rows = matmul_high(inverse, values * beta[..., None])
    final_decay = log_decay[..., -1:]
    tail_keys = keys * jnp.exp(final_decay - log_decay)[..., None]
    identity_key = jnp.eye(keys.shape[-1], dtype=jnp.float32)
    carry_map = jnp.exp(final_decay)[..., None] * identity_key - jnp.einsum(
        "...id,...ie->...de", w_rows, tail_keys, precision=HIGHEST
    )
    carry_add = jnp.einsum("...iv,...ie->...ve", u_rows, tail_keys, precision=HIGHEST)
    base = jnp.einsum("...ij,...jv->...iv", scores, u_rows, precision=HIGHEST)
    probe = query * growth[..., None] - jnp.einsum(
        "...ij,...jd->...id", scores, w_rows, precision=HIGHEST
    )
    return (base, probe, carry_map, carry_add)


def causal_mix(inputs, tail, taps, within, slot_starts):
    depth = taps.shape[0]
    row_count = inputs.shape[0]
    extended = jnp.concatenate([tail, inputs], axis=0).astype(jnp.float32)
    weights = taps.astype(jnp.float32)
    total = extended[depth - 1 :] * weights[depth - 1]
    for offset in range(1, depth):
        moved = extended[depth - 1 - offset : depth - 1 - offset + row_count]
        keeping = jnp.logical_not((within < offset) & slot_starts)
        total = total + jnp.where(keeping[:, None], moved, 0.0) * weights[depth - 1 - offset]
    return jax.nn.silu(total)


def link(earlier, later):
    early_map, early_add, early_flag = earlier
    late_map, late_add, late_flag = later
    resetting = late_flag > 0.5
    joined_map = jnp.where(resetting, late_map, matmul_high(early_map, late_map))
    joined_add = jnp.where(resetting, late_add, matmul_high(early_add, late_map) + late_add)
    return (joined_map, joined_add, jnp.maximum(early_flag, late_flag))


def swiglu(inputs, gate_rows, up_rows):
    gate_part = jnp.einsum("rd,fd->rf", inputs, gate_rows, preferred_element_type=jnp.float32)
    up_part = jnp.einsum("rd,fd->rf", inputs, up_rows, preferred_element_type=jnp.float32)
    return (jax.nn.silu(gate_part) * up_part).astype(jnp.bfloat16)


def per_device(
    tokens,
    stretch_prompt,
    last_fill,
    ln1_gain,
    w_qk,
    w_vz,
    w_ba,
    conv_qk,
    conv_value,
    decay_log,
    dt_bias,
    norm_gain,
    w_out,
    ln2_gain,
    w_sgate,
    shared_weights,
):
    model_width = tokens.shape[1]
    weight_qk = w_qk.reshape(model_width, -1)
    weight_vz = w_vz.reshape(model_width, -1)
    weight_ba = w_ba.reshape(model_width, -1)
    width_qk = weight_qk.shape[1]
    width_vz = weight_vz.shape[1]
    half_vz = width_vz // 2
    normed = scaled_rows(tokens, ln1_gain).astype(jnp.bfloat16)
    piece = lax.all_gather(normed, "head", axis=0, tiled=True)
    outputs = [
        jnp.dot(piece, weight, preferred_element_type=jnp.float32)
        for weight in (weight_qk, weight_vz, weight_ba)
    ]
    projected = jnp.concatenate(outputs, axis=1).astype(jnp.bfloat16)
    group_rows = projected.shape[0]
    proj_qk = projected[:, :width_qk]
    proj_value = projected[:, width_qk : width_qk + half_vz]
    proj_gate = projected[:, width_qk + half_vz : width_qk + width_vz]
    proj_ba = projected[:, width_qk + width_vz :].astype(jnp.float32)
    device = lax.axis_index("dp")
    first_slot = device * SLOTS
    before = jnp.concatenate([jnp.full((1,), -1, jnp.int32), stretch_prompt])
    after = jnp.concatenate([stretch_prompt, jnp.full((1,), -1, jnp.int32)])
    current = lax.dynamic_slice_in_dim(stretch_prompt, first_slot, SLOTS)
    starts = current != lax.dynamic_slice_in_dim(before, first_slot, SLOTS)
    ends = current != lax.dynamic_slice_in_dim(after, first_slot + 1, SLOTS)
    fill = jnp.where(ends, lax.dynamic_slice_in_dim(last_fill, first_slot, SLOTS), STRETCH)
    depth = conv_qk.shape[0]
    tail_qk, tail_value = shifted(
        (proj_qk[group_rows - depth + 1 :], proj_value[group_rows - depth + 1 :]), "dp", 1
    )
    within = jnp.arange(group_rows) % STRETCH
    slot_starts = jnp.repeat(starts, STRETCH)
    mixed_qk = causal_mix(proj_qk, tail_qk, conv_qk.reshape(depth, -1), within, slot_starts)
    mixed_value = causal_mix(proj_value, tail_value, conv_value, within, slot_starts)
    keys_local = width_qk // (2 * DK)
    heads_local = half_vz // DV
    groups = heads_local // keys_local
    query = unit_rows(mixed_qk[:, : keys_local * DK].reshape(group_rows, keys_local, DK)) * DK ** (
        -0.5
    )
    keys = unit_rows(mixed_qk[:, keys_local * DK :].reshape(group_rows, keys_local, DK))
    values = mixed_value.reshape(group_rows, heads_local, DV)
    beta = jax.nn.sigmoid(proj_ba[:, :heads_local])
    rate = -jnp.exp(decay_log) * jax.nn.softplus(proj_ba[:, heads_local:] + dt_bias)
    block_count = group_rows // BLOCK
    per_stretch = STRETCH // BLOCK

    def to_blocks(array):
        shaped = array.reshape((block_count, BLOCK) + array.shape[1:])
        return jnp.moveaxis(shaped, 2, 0)

    base, probe, carry_map, carry_add = block_terms(
        to_blocks(jnp.repeat(query, groups, axis=1)),
        to_blocks(jnp.repeat(keys, groups, axis=1)),
        to_blocks(values),
        to_blocks(beta),
        to_blocks(rate),
    )

    def split_stretches(array):
        shaped = array.reshape((heads_local, SLOTS, per_stretch) + array.shape[2:])
        return jnp.moveaxis(shaped, 2, 0)

    block_maps = split_stretches(carry_map)
    block_adds = split_stretches(carry_add)
    identity_key = jnp.eye(DK, dtype=jnp.float32)
    start_maps = (
        jnp.broadcast_to(identity_key, (heads_local, SLOTS, DK, DK)),
        jnp.zeros((heads_local, SLOTS, DV, DK), jnp.float32),
    )

    def compose(carry, item):
        lead_map, lead_add = carry
        step_map, step_add = item
        return ((matmul_high(lead_map, step_map), matmul_high(lead_add, step_map) + step_add), None)

    (stretch_map, stretch_add), unused = lax.scan(compose, start_maps, (block_maps, block_adds))
    fresh = starts.astype(jnp.float32)
    element = (stretch_map[:, 0], stretch_add[:, 0], fresh[0])
    slot_index = 1
    element = link(
        element, (stretch_map[:, slot_index], stretch_add[:, slot_index], fresh[slot_index])
    )

    def relay(counter, arriving):
        leaving = jnp.where(
            element[2] > 0.5, element[1], matmul_high(arriving, element[0]) + element[1]
        )
        return shifted(leaving.astype(jnp.bfloat16), "dp", 1).astype(leaving.dtype)

    entering = lax.fori_loop(0, lax.axis_size("dp") - 1, relay, jnp.zeros_like(element[1]))
    running = entering
    openings = []
    for slot_index in range(SLOTS):
        opening = jnp.where(starts[slot_index], 0.0, running)
        openings.append(opening)
        if slot_index + 1 < SLOTS:
            running = matmul_high(opening, stretch_map[:, slot_index]) + stretch_add[:, slot_index]
    stacked = jnp.stack(openings, axis=1)

    def walk(state, item):
        step_map, step_add = item
        return (matmul_high(state, step_map) + step_add, state)

    unused_state, block_state = lax.scan(walk, stacked, (block_maps, block_adds))
    block_state = jnp.moveaxis(block_state, 0, 2).reshape(heads_local, block_count, DV, DK)
    recurrent = base + jnp.einsum("...id,...vd->...iv", probe, block_state, precision=HIGHEST)
    recurrent = jnp.moveaxis(recurrent, 0, 2).reshape(group_rows, heads_local, DV)
    kept = (jnp.arange(STRETCH)[None, :] < fill[:, None]).reshape(group_rows)
    recurrent = jnp.where(kept[:, None, None], recurrent, 0.0)
    gating = proj_gate.astype(jnp.float32).reshape(group_rows, heads_local, DV)
    gated = (
        (scaled_rows(recurrent, norm_gain) * jax.nn.silu(gating))
        .reshape(group_rows, heads_local * DV)
        .astype(jnp.bfloat16)
    )
    attention_out = lax.psum_scatter(
        jnp.dot(gated, w_out, preferred_element_type=jnp.float32).astype(jnp.bfloat16),
        "head",
        scatter_dimension=0,
        tiled=True,
    )
    residual = (tokens.astype(jnp.float32) + attention_out.astype(jnp.float32)).astype(jnp.bfloat16)
    normed_two = scaled_rows(residual, ln2_gain).astype(jnp.bfloat16)
    expert_gate = jax.nn.sigmoid(jnp.dot(normed_two, w_sgate, preferred_element_type=jnp.float32))
    gathered = lax.all_gather(shared_weights, "head", axis=1, tiled=True)
    hidden = swiglu(normed_two, gathered[0], gathered[1])
    expert = jnp.dot(hidden, gathered[2], preferred_element_type=jnp.float32)
    layer_out = (residual.astype(jnp.float32) + expert_gate[:, None] * expert).astype(jnp.bfloat16)
    return (attention_out, layer_out)


def solution(mesh):
    return jax.shard_map(
        per_device,
        mesh=mesh,
        in_specs=(
            P(("dp", "head"), None),
            P(),
            P(),
            P(),
            P(None, None, "head"),
            P(None, None, "head"),
            P(None, None, "head"),
            P(None, None, "head"),
            P(None, "head"),
            P("head"),
            P("head"),
            P(),
            P("head", None),
            P(),
            P(),
            P(None, "head", None),
        ),
        out_specs=(P(("dp", "head"), None), P(("dp", "head"), None)),
        check_vma=False,
    )
```

profile of v0, /device:TPU:1, one launch (start us, length us, event | category | flops | bytes accessed | tf_op | source)
XLA Modules:
  0.0 743.0 jit_solution(11275923519735953908)
XLA Ops:
  23.2 27.2 %all-gather.3.cloned.1.call-done = bf16[1024,2048]{1,0:T(8,128)(2,1)} async-done(((bf16[128,2048]{1,0:T(8,128)(2,1)}), bf16[1024,2048]{1,0:T(8,128)(2,1)}) %all-gather.3.cloned.1.call-update) | async-done | bytes 4194320 | tf_op jit(solution)/shard_map/all_gather | solution.py:134
  50.4 8.1 %convolution_convert_fusion.1 = bf16[1024,1024]{1,0:T(8,128)(2,1)S(1)} fusion(bf16[1024,2048]{1,0:T(8,128)(2,1)} %all-gather.3.cloned.1.call-done, bf16[2048,1024]{1,0:T(8,128)(2,1)} %bitcast.224), kind=kOutput, calls=%fused_computation.97 | convolution fusion | flops 4296015872 | bytes 10485760 | tf_op jit(solution)/shard_map/dot_general | solution.py:136
  148.7 9.0 %fusion.63 = f32[4,16,128,128]{3,2,1,0:T(8,128)} fusion(f32[4,16,64,128]{3,2,1,0:T(8,128)S(1)} %fusion.45, f32[4,16,64,128]{3,2,1,0:T(8,128)S(1)} %bitcast.215, f32[4,16,64]{2,1,0:T(8,128)S(1)} %get-tuple-element.211), kind=kOutput, calls=%fused_computation.94 | convolution fusion | flops 805830656 | bytes 8404992 | tf_op jit(solution)/shard_map/...iv,...ie->...ve/dot_general | solution.py:72
  163.4 12.1 %multiply_subtract_fusion = f32[4,16,128,128]{3,2,1,0:T(8,128)} fusion(f32[4,16,64,128]{3,2,1,0:T(8,128)} %copy-done.4, f32[128,128]{1,0:T(8,128)S(1)} %fusion.126, f32[4,16]{1,0:T(4,128)S(1)} %get-tuple-element.174, f32[4,16,64,128]{3,2,1,0:T(8,128)} %bitcast.212, f32[4,16,64]{2,1,0:T(8,128)S(1)} %get-tuple-element.211), kind=kOutput, calls=%fused_computation.26 | convolution fusion | flops 807927808 | bytes 8470784 | tf_op jit(solution)/shard_map/...id,...ie->...de/dot_general | solution.py:69
  181.0 29.4 %while.39 = (s32[]{:T(128)}, f32[4,2,128,128]{2,3,1,0:T(8,128)S(1)}, f32[4,2,128,128]{2,3,1,0:T(8,128)S(1)}, f32[8,4,2,128,128]{3,4,2,1,0:T(8,128)}, f32[8,4,2,128,128]{3,4,2,1,0:T(8,128)}, /*index=5*/s32[]{:T(128)}, s32[]{:T(128)}) while((s32[]{:T(128)}, f32[4,2,128,128]{2,3,1,0:T(8,128)S(1)}, f32[4,2,128,128]{2,3,1,0:T(8,128)S(1)}, ...), condition=%wide.region_4.5_spmd.clone, body=%wide.region_3.4_spmd.clone.sunk | while | flops 402915328 | bytes 5768791 | solution.py:203
  215.4 280.5 %while.40 = (s32[]{:T(128)}, f32[4,128,128]{2,1,0:T(8,128)S(1)}, pred[]{:T(512)}, f32[4,128,128]{2,1,0:T(8,128)S(1)}, f32[4,128,128]{2,1,0:T(8,128)S(1)}, /*index=5*/s32[]{:T(128)}, s32[]{:T(128)}) while((s32[]{:T(128)}, f32[4,128,128]{2,1,0:T(8,128)S(1)}, pred[]{:T(512)}, f32[4,128,128]{2,1,0:T(8,128)S(1)}, ...), condition=%wide.region_6.7_spmd.clone, body=%wide.region_5.6_spmd.clone.sunk | while | flops 100990976 | bytes 1835136 | solution.py:217
  252.5 5.8 collective-permute-start
  280.3 6.1 collective-permute-start
  290.9 5.9 collective-permute-start
  300.2 5.9 collective-permute-start
  309.4 5.8 collective-permute-start
  318.6 6.1 collective-permute-start
  328.1 5.8 collective-permute-start
  364.7 6.0 collective-permute-start
  375.1 6.4 collective-permute-start
  402.9 6.1 collective-permute-start
  412.4 5.8 collective-permute-start
  459.0 6.3 collective-permute-start
  469.5 5.9 collective-permute-start
  487.4 6.1 collective-permute-start
  500.3 38.1 %while.38 = (s32[]{:T(128)}, f32[4,2,128,128]{2,3,1,0:T(8,128)}, f32[8,4,2,128,128]{4,3,0,2,1:T(8,128)}, f32[8,4,2,128,128]{3,4,2,1,0:T(8,128)}, f32[8,4,2,128,128]{3,4,2,1,0:T(8,128)}, /*index=5*/s32[]{:T(128)}) while((s32[]{:T(128)}, f32[4,2,128,128]{2,3,1,0:T(8,128)}, f32[8,4,2,128,128]{4,3,0,2,1:T(8,128)}, ...), condition=%wide.region_8.9_spmd, body=%wide.region_7.8_spmd.sunk | while | flops 201457664 | bytes 5244485 | solution.py:231
  538.4 13.5 %multiply_reduce_fusion = (f32[16,64,4]{1,0,2:T(8,128)S(1)}, f32[16,64,4,128]{3,1,0,2:T(8,128)}) fusion(pred[16,64]{1,0:T(8,128)(4,1)S(1)} %broadcast_compare_fusion, f32[4,16,64,128]{3,2,1,0:T(8,128)} %fusion.162, f32[4,16,128,128]{3,2,1,0:T(8,128)} %bitcast.223, f32[4,16,64,128]{3,2,1,0:T(8,128)} %fusion.163, f32[4,16,64,128]{3,2,1,0:T(8,128)} %bitcast.219, ...), kind=kOutput, calls=%fused_computation.72 | convolution fusion | flops 808448000 | bytes 12616704 | tf_op jit(solution)/shard_map/...id,...vd->...iv/dot_general | solution.py:233
  562.3 119.6 %reduce-scatter.2.cloned.1.call-done = bf16[128,2048]{1,0:T(8,128)(2,1)} async-done(((bf16[1024,2048]{1,0:T(8,128)(2,1)}), bf16[128,2048]{1,0:T(8,128)(2,1)}) %reduce-scatter.2.cloned.1.call-update) | async-done | bytes 524304 | tf_op jit(solution)/shard_map/reduce_scatter | solution.py:243
  683.5 46.0 %all-gather.5.cloned.1.call-done = bf16[3,512,2048]{2,1,0:T(8,128)(2,1)} async-done(((bf16[3,64,2048]{2,1,0:T(8,128)(2,1)}), bf16[3,512,2048]{2,1,0:T(8,128)(2,1)}) %all-gather.5.cloned.1.call-update) | async-done | bytes 6291472 | tf_op jit(solution)/shard_map/all_gather | solution.py:252
  (351 shorter events, 405.3 us)
Async XLA Ops:
  7.2 43.2 %all-gather.3.cloned.1.call-start = ((), (), s32[]{:S(2)}) async-start(), calls=%async_computation.1 | async-start | bytes 4718592 | tf_op jit(solution)/shard_map/all_gather | solution.py:134
  11.4 670.5 %reduce-scatter.2.cloned.1.call-start = ((), (), s32[]{:S(2)}) async-start(), calls=%async_computation.2 | async-start | bytes 4718592 | tf_op jit(solution)/shard_map/reduce_scatter | solution.py:243
  58.5 12.5 %collective-permute-start.2 = (bf16[3,512]{1,0:T(4,128)(2,1)S(1)}, bf16[3,512]{1,0:T(4,128)(2,1)S(1)}, u32[]{:S(2)}, u32[]{:S(2)}) collective-permute-start(bf16[3,512]{1,0:T(4,128)(2,1)S(1)} %slice.177), channel_id=1, source_target_pairs={{0,8},{8,16},{16,24},{24,32},{32,40},{40,48},{48,56},{56,64},{64,7... | collective-permute-start | bytes 9224 | tf_op jit(solution)/shard_map/ppermute | solution.py:20
  252.5 8.0 %collective-permute-start = (bf16[4,128,128]{2,1,0:T(8,128)(2,1)}, bf16[4,128,128]{2,1,0:T(8,128)(2,1)S(1)}, u32[]{:S(2)}, u32[]{:S(2)}) collective-permute-start(bf16[4,128,128]{2,1,0:T(8,128)(2,1)} %fusion.222), channel_id=1, source_target_pairs={{0,8},{8,16},{16,24},{24,32},{32,40},{40,48},{48,56},{56,64},{64,7... | collective-permute-start | bytes 393224 | tf_op jit(solution)/shard_map/while/body/eval_jaxpr/ppermute | solution.py:20
  261.6 8.0 %collective-permute-start = (bf16[4,128,128]{2,1,0:T(8,128)(2,1)}, bf16[4,128,128]{2,1,0:T(8,128)(2,1)S(1)}, u32[]{:S(2)}, u32[]{:S(2)}) collective-permute-start(bf16[4,128,128]{2,1,0:T(8,128)(2,1)} %fusion.222), channel_id=1, source_target_pairs={{0,8},{8,16},{16,24},{24,32},{32,40},{40,48},{48,56},{56,64},{64,7... | collective-permute-start | bytes 393224 | tf_op jit(solution)/shard_map/while/body/eval_jaxpr/ppermute | solution.py:20
  270.8 8.4 %collective-permute-start = (bf16[4,128,128]{2,1,0:T(8,128)(2,1)}, bf16[4,128,128]{2,1,0:T(8,128)(2,1)S(1)}, u32[]{:S(2)}, u32[]{:S(2)}) collective-permute-start(bf16[4,128,128]{2,1,0:T(8,128)(2,1)} %fusion.222), channel_id=1, source_target_pairs={{0,8},{8,16},{16,24},{24,32},{32,40},{40,48},{48,56},{56,64},{64,7... | collective-permute-start | bytes 393224 | tf_op jit(solution)/shard_map/while/body/eval_jaxpr/ppermute | solution.py:20
  280.3 9.5 %collective-permute-start = (bf16[4,128,128]{2,1,0:T(8,128)(2,1)}, bf16[4,128,128]{2,1,0:T(8,128)(2,1)S(1)}, u32[]{:S(2)}, u32[]{:S(2)}) collective-permute-start(bf16[4,128,128]{2,1,0:T(8,128)(2,1)} %fusion.222), channel_id=1, source_target_pairs={{0,8},{8,16},{16,24},{24,32},{32,40},{40,48},{48,56},{56,64},{64,7... | collective-permute-start | bytes 393224 | tf_op jit(solution)/shard_map/while/body/eval_jaxpr/ppermute | solution.py:20
  290.9 8.2 %collective-permute-start = (bf16[4,128,128]{2,1,0:T(8,128)(2,1)}, bf16[4,128,128]{2,1,0:T(8,128)(2,1)S(1)}, u32[]{:S(2)}, u32[]{:S(2)}) collective-permute-start(bf16[4,128,128]{2,1,0:T(8,128)(2,1)} %fusion.222), channel_id=1, source_target_pairs={{0,8},{8,16},{16,24},{24,32},{32,40},{40,48},{48,56},{56,64},{64,7... | collective-permute-start | bytes 393224 | tf_op jit(solution)/shard_map/while/body/eval_jaxpr/ppermute | solution.py:20
  300.2 8.1 %collective-permute-start = (bf16[4,128,128]{2,1,0:T(8,128)(2,1)}, bf16[4,128,128]{2,1,0:T(8,128)(2,1)S(1)}, u32[]{:S(2)}, u32[]{:S(2)}) collective-permute-start(bf16[4,128,128]{2,1,0:T(8,128)(2,1)} %fusion.222), channel_id=1, source_target_pairs={{0,8},{8,16},{16,24},{24,32},{32,40},{40,48},{48,56},{56,64},{64,7... | collective-permute-start | bytes 393224 | tf_op jit(solution)/shard_map/while/body/eval_jaxpr/ppermute | solution.py:20
  309.4 8.1 %collective-permute-start = (bf16[4,128,128]{2,1,0:T(8,128)(2,1)}, bf16[4,128,128]{2,1,0:T(8,128)(2,1)S(1)}, u32[]{:S(2)}, u32[]{:S(2)}) collective-permute-start(bf16[4,128,128]{2,1,0:T(8,128)(2,1)} %fusion.222), channel_id=1, source_target_pairs={{0,8},{8,16},{16,24},{24,32},{32,40},{40,48},{48,56},{56,64},{64,7... | collective-permute-start | bytes 393224 | tf_op jit(solution)/shard_map/while/body/eval_jaxpr/ppermute | solution.py:20
  318.6 8.3 %collective-permute-start = (bf16[4,128,128]{2,1,0:T(8,128)(2,1)}, bf16[4,128,128]{2,1,0:T(8,128)(2,1)S(1)}, u32[]{:S(2)}, u32[]{:S(2)}) collective-permute-start(bf16[4,128,128]{2,1,0:T(8,128)(2,1)} %fusion.222), channel_id=1, source_target_pairs={{0,8},{8,16},{16,24},{24,32},{32,40},{40,48},{48,56},{56,64},{64,7... | collective-permute-start | bytes 393224 | tf_op jit(solution)/shard_map/while/body/eval_jaxpr/ppermute | solution.py:20
  328.1 8.0 %collective-permute-start = (bf16[4,128,128]{2,1,0:T(8,128)(2,1)}, bf16[4,128,128]{2,1,0:T(8,128)(2,1)S(1)}, u32[]{:S(2)}, u32[]{:S(2)}) collective-permute-start(bf16[4,128,128]{2,1,0:T(8,128)(2,1)} %fusion.222), channel_id=1, source_target_pairs={{0,8},{8,16},{16,24},{24,32},{32,40},{40,48},{48,56},{56,64},{64,7... | collective-permute-start | bytes 393224 | tf_op jit(solution)/shard_map/while/body/eval_jaxpr/ppermute | solution.py:20
  346.4 8.0 %collective-permute-start = (bf16[4,128,128]{2,1,0:T(8,128)(2,1)}, bf16[4,128,128]{2,1,0:T(8,128)(2,1)S(1)}, u32[]{:S(2)}, u32[]{:S(2)}) collective-permute-start(bf16[4,128,128]{2,1,0:T(8,128)(2,1)} %fusion.222), channel_id=1, source_target_pairs={{0,8},{8,16},{16,24},{24,32},{32,40},{40,48},{48,56},{56,64},{64,7... | collective-permute-start | bytes 393224 | tf_op jit(solution)/shard_map/while/body/eval_jaxpr/ppermute | solution.py:20
  355.6 8.0 %collective-permute-start = (bf16[4,128,128]{2,1,0:T(8,128)(2,1)}, bf16[4,128,128]{2,1,0:T(8,128)(2,1)S(1)}, u32[]{:S(2)}, u32[]{:S(2)}) collective-permute-start(bf16[4,128,128]{2,1,0:T(8,128)(2,1)} %fusion.222), channel_id=1, source_target_pairs={{0,8},{8,16},{16,24},{24,32},{32,40},{40,48},{48,56},{56,64},{64,7... | collective-permute-start | bytes 393224 | tf_op jit(solution)/shard_map/while/body/eval_jaxpr/ppermute | solution.py:20
  364.7 9.3 %collective-permute-start = (bf16[4,128,128]{2,1,0:T(8,128)(2,1)}, bf16[4,128,128]{2,1,0:T(8,128)(2,1)S(1)}, u32[]{:S(2)}, u32[]{:S(2)}) collective-permute-start(bf16[4,128,128]{2,1,0:T(8,128)(2,1)} %fusion.222), channel_id=1, source_target_pairs={{0,8},{8,16},{16,24},{24,32},{32,40},{40,48},{48,56},{56,64},{64,7... | collective-permute-start | bytes 393224 | tf_op jit(solution)/shard_map/while/body/eval_jaxpr/ppermute | solution.py:20
  375.1 9.1 %collective-permute-start = (bf16[4,128,128]{2,1,0:T(8,128)(2,1)}, bf16[4,128,128]{2,1,0:T(8,128)(2,1)S(1)}, u32[]{:S(2)}, u32[]{:S(2)}) collective-permute-start(bf16[4,128,128]{2,1,0:T(8,128)(2,1)} %fusion.222), channel_id=1, source_target_pairs={{0,8},{8,16},{16,24},{24,32},{32,40},{40,48},{48,56},{56,64},{64,7... | collective-permute-start | bytes 393224 | tf_op jit(solution)/shard_map/while/body/eval_jaxpr/ppermute | solution.py:20
  402.9 8.3 %collective-permute-start = (bf16[4,128,128]{2,1,0:T(8,128)(2,1)}, bf16[4,128,128]{2,1,0:T(8,128)(2,1)S(1)}, u32[]{:S(2)}, u32[]{:S(2)}) collective-permute-start(bf16[4,128,128]{2,1,0:T(8,128)(2,1)} %fusion.222), channel_id=1, source_target_pairs={{0,8},{8,16},{16,24},{24,32},{32,40},{40,48},{48,56},{56,64},{64,7... | collective-permute-start | bytes 393224 | tf_op jit(solution)/shard_map/while/body/eval_jaxpr/ppermute | solution.py:20
  412.4 8.0 %collective-permute-start = (bf16[4,128,128]{2,1,0:T(8,128)(2,1)}, bf16[4,128,128]{2,1,0:T(8,128)(2,1)S(1)}, u32[]{:S(2)}, u32[]{:S(2)}) collective-permute-start(bf16[4,128,128]{2,1,0:T(8,128)(2,1)} %fusion.222), channel_id=1, source_target_pairs={{0,8},{8,16},{16,24},{24,32},{32,40},{40,48},{48,56},{56,64},{64,7... | collective-permute-start | bytes 393224 | tf_op jit(solution)/shard_map/while/body/eval_jaxpr/ppermute | solution.py:20
  430.7 8.0 %collective-permute-start = (bf16[4,128,128]{2,1,0:T(8,128)(2,1)}, bf16[4,128,128]{2,1,0:T(8,128)(2,1)S(1)}, u32[]{:S(2)}, u32[]{:S(2)}) collective-permute-start(bf16[4,128,128]{2,1,0:T(8,128)(2,1)} %fusion.222), channel_id=1, source_target_pairs={{0,8},{8,16},{16,24},{24,32},{32,40},{40,48},{48,56},{56,64},{64,7... | collective-permute-start | bytes 393224 | tf_op jit(solution)/shard_map/while/body/eval_jaxpr/ppermute | solution.py:20
  449.0 8.9 %collective-permute-start = (bf16[4,128,128]{2,1,0:T(8,128)(2,1)}, bf16[4,128,128]{2,1,0:T(8,128)(2,1)S(1)}, u32[]{:S(2)}, u32[]{:S(2)}) collective-permute-start(bf16[4,128,128]{2,1,0:T(8,128)(2,1)} %fusion.222), channel_id=1, source_target_pairs={{0,8},{8,16},{16,24},{24,32},{32,40},{40,48},{48,56},{56,64},{64,7... | collective-permute-start | bytes 393224 | tf_op jit(solution)/shard_map/while/body/eval_jaxpr/ppermute | solution.py:20
  459.0 9.4 %collective-permute-start = (bf16[4,128,128]{2,1,0:T(8,128)(2,1)}, bf16[4,128,128]{2,1,0:T(8,128)(2,1)S(1)}, u32[]{:S(2)}, u32[]{:S(2)}) collective-permute-start(bf16[4,128,128]{2,1,0:T(8,128)(2,1)} %fusion.222), channel_id=1, source_target_pairs={{0,8},{8,16},{16,24},{24,32},{32,40},{40,48},{48,56},{56,64},{64,7... | collective-permute-start | bytes 393224 | tf_op jit(solution)/shard_map/while/body/eval_jaxpr/ppermute | solution.py:20
  469.5 8.1 %collective-permute-start = (bf16[4,128,128]{2,1,0:T(8,128)(2,1)}, bf16[4,128,128]{2,1,0:T(8,128)(2,1)S(1)}, u32[]{:S(2)}, u32[]{:S(2)}) collective-permute-start(bf16[4,128,128]{2,1,0:T(8,128)(2,1)} %fusion.222), channel_id=1, source_target_pairs={{0,8},{8,16},{16,24},{24,32},{32,40},{40,48},{48,56},{56,64},{64,7... | collective-permute-start | bytes 393224 | tf_op jit(solution)/shard_map/while/body/eval_jaxpr/ppermute | solution.py:20
  487.4 8.3 %collective-permute-start = (bf16[4,128,128]{2,1,0:T(8,128)(2,1)}, bf16[4,128,128]{2,1,0:T(8,128)(2,1)S(1)}, u32[]{:S(2)}, u32[]{:S(2)}) collective-permute-start(bf16[4,128,128]{2,1,0:T(8,128)(2,1)} %fusion.222), channel_id=1, source_target_pairs={{0,8},{8,16},{16,24},{24,32},{32,40},{40,48},{48,56},{56,64},{64,7... | collective-permute-start | bytes 393224 | tf_op jit(solution)/shard_map/while/body/eval_jaxpr/ppermute | solution.py:20
  561.5 168.0 %all-gather.5.cloned.1.call-start = ((), (), s32[]{:S(2)}) async-start(), calls=%async_computation.3 | async-start | bytes 7077888 | tf_op jit(solution)/shard_map/all_gather | solution.py:252
  (43 other events, 1246.4 us)
Sparse Core Ops, SparseCore 0:
  11.5 38.8 all-gather.2
  561.6 120.1 reduce-scatter.1
  683.7 45.7 all-gather.4
where the time goes:
time: 751 us; the launch traced here: 743 us
  waiting for transfers between devices  268 us (36%)
  matrix products  197 us (26%)
  starting transfers between devices  178 us (24%)
  local copies, waits for them, and re-layouts  58.5 us (8%)
  other arithmetic  24.2 us (3%)
  between operations  16.7 us (2%)
    ppermute x33, starting transfers between devices, shifted(): lax.ppermute(value, axis, [(source, source + steps) for source in range(f...  178 us
    dot_general x70, matrix products, matmul_high(): return jnp.einsum('...ij,...jk->...ik', left, right, precision=HIGHEST)  123 us
    reduce_scatter x1, waiting for transfers between devices, per_device(): lax.psum_scatter(jnp.dot(gated, w_out, preferred_element_type=jnp.float32...  120 us
    ppermute x33, waiting for transfers between devices, shifted(): lax.ppermute(value, axis, [(source, source + steps) for source in range(f...  74.1 us
    all_gather x1, waiting for transfers between devices, per_device(): gathered = lax.all_gather(shared_weights, 'head', axis=1, tiled=True)  46 us
    all_gather x1, waiting for transfers between devices, per_device(): piece = lax.all_gather(normed, 'head', axis=0, tiled=True)  27.2 us
  transfers between devices with their start and end apart: 36, of which 34 were waited for; matrix products, arithmetic and copies ran while one was open for 2% of the time, Pallas kernels for 0%

commit v1 on v0

v1 whole, which is shorter than its diff:
```python
import jax
import jax.numpy as jnp
from jax import lax
from jax.experimental import pallas as pl
from jax.experimental.pallas import tpu as pltpu
from jax.sharding import Mesh
from jax.sharding import PartitionSpec as P

F32 = jnp.float32
BF16 = jnp.bfloat16
EPSILON = 1e-06
DK = 128
STRETCH = 512
ROWS = 128
CHUNKS = 8
HEADS = 4
KEYS = 2
NZ, NX, NY, NC = 8, 4, 4, 2
LEAD = 16
COL_V = 256
COL_Q = 768
COL_BA = 1024
COL_Z = 1152
COL_END = 1664
PLACES = {
    (0, 0): (0, 0),
    (0, 1): (0, 1),
    (1, 0): (1, 0),
    (3, 0): (1, 1),
    (1, 1): (1, 2),
    (3, 1): (1, 3),
    (2, 0): (2, 0),
    (2, 1): (2, 1),
}


def dot(left, right, contract=((1,), (0,))):
    return lax.dot_general(left, right, (contract, ((), ())), preferred_element_type=F32)


def silu(value):
    return value * (0.5 * jnp.tanh(0.5 * value) + 0.5)


def sigmoid(value):
    return 0.5 * jnp.tanh(0.5 * value) + 0.5


def scaled_rows(inputs, scaling):
    widened = inputs.astype(F32)
    spread = jnp.mean(widened * widened, axis=-1, keepdims=True)
    return widened * lax.rsqrt(spread + EPSILON) * scaling.astype(F32)


def turn(value, axis, steps, count):
    return lax.ppermute(value, axis, [(i, (i + steps) % count) for i in range(count)])


def push(value, axis, steps, count):
    return lax.ppermute(value, axis, [(i, i + steps) for i in range(count - steps)])


def mixed_rows(ref, chunk, first, last, taps, reset):
    start = pl.multiple_of(chunk * ROWS, ROWS)
    rows = ref[pl.ds(start, ROWS + LEAD), first:last].astype(F32)
    lead = jnp.where(reset, 0.0, rows[:LEAD])
    rows = jnp.concatenate([lead, rows[LEAD:]], axis=0)
    total = rows[LEAD:] * taps[3:4]
    for offset in (1, 2, 3):
        total = total + rows[LEAD - offset : LEAD - offset + ROWS] * taps[3 - offset : 4 - offset]
    return silu(total)


def unit_heads(value):
    parts = []
    for head in range(value.shape[1] // DK):
        part = value[:, head * DK : (head + 1) * DK]
        parts.append(part * lax.rsqrt(jnp.sum(part * part, axis=-1, keepdims=True) + EPSILON))
    return parts


def fetch_rows(scal, pieces, scratch, sems, first, last):
    copies = []
    for place, ((steps, other), (piece, block)) in enumerate(PLACES.items()):
        row = lax.rem(scal[0] + steps, NY)
        core = scal[1] if other == 0 else 1 - scal[1]
        chunk = row * NC + core
        start = pl.multiple_of(chunk * ROWS + LEAD, LEAD)
        copy = pltpu.make_async_copy(
            pieces[piece].at[pl.ds(block * ROWS, ROWS), pl.ds(first, last - first)],
            scratch.at[pl.ds(start, ROWS), :],
            sems.at[place],
        )
        copy.start()
        copies.append(copy)
    for copy in copies:
        copy.wait()


def is_reset(scal, chunk):
    first = jnp.logical_and(chunk == 0, scal[2] > 0)
    second = jnp.logical_and(chunk == CHUNKS // 2, scal[3] > 0)
    return jnp.logical_or(first, second)


def iota2(axis):
    return lax.broadcasted_iota(jnp.int32, (ROWS, ROWS), axis)


def inverse_rest(strict):
    row, col = iota2(0), iota2(1)
    near = jnp.logical_and(row // 2 == col // 2, row != col)
    rest = jnp.where(near, -strict, 0.0)
    span = 2
    while span < ROWS:
        wide = 2 * span
        inside = (row // wide == col // wide) & (row % wide >= span) & (col % wide < span)
        below = jnp.where(inside, strict, 0.0)
        half = below + dot(below.astype(BF16), rest.astype(BF16))
        rest = rest - half - dot(rest.astype(BF16), half.astype(BF16))
        span = wide
    return rest


def state_kernel(
    scal, piece_a, piece_b, piece_c, tail, taps, decay, bias,
    xend, xs, vs, khat, logs, raw, rest, kturn, values, betas, state, sems,
):
    raw[0:LEAD, :] = tail[...]
    fetch_rows(scal, (piece_a, piece_b, piece_c), raw, sems, 0, COL_Z)
    row, col = iota2(0), iota2(1)
    strict = row > col
    summing = (row >= col).astype(F32)

    def prepare(chunk):
        reset = is_reset(scal, chunk)
        mixed = mixed_rows(raw, chunk, 0, COL_Q, taps, reset)
        start = pl.multiple_of(chunk * ROWS + LEAD, LEAD)
        ba = raw[pl.ds(start, ROWS), COL_BA:COL_Z].astype(F32)
        beta = sigmoid(ba)
        inner = ba + bias[...]
        soft = jnp.maximum(inner, 0.0) + jnp.log1p(jnp.exp(-jnp.abs(inner)))
        rate = -jnp.exp(decay[...]) * soft
        log = lax.dot_general(
            summing, rate, (((1,), (0,)), ((), ())),
            precision=lax.Precision.HIGHEST, preferred_element_type=F32,
        )
        log_turned = log.T
        betas[chunk] = beta
        logs[chunk] = log
        unit = unit_heads(mixed[:, :COL_V])
        for key in range(KEYS):
            key_rows = unit[key].astype(BF16)
            khat[chunk, key] = key_rows
            kturn[chunk, key] = unit[key].T.astype(BF16)
            products = dot(key_rows, key_rows, ((1,), (1,)))
            for half in range(2):
                head = 2 * key + half
                beta_col = beta[:, head : head + 1]
                spread = log[:, HEADS + head : HEADS + head + 1] - log_turned[HEADS + head : HEADS + head + 1, :]
                weight = jnp.exp(jnp.minimum(spread, 0.0))
                lower = jnp.where(strict, products * beta_col * weight, 0.0)
                rest[chunk, head] = inverse_rest(lower).astype(BF16)
                value = mixed[:, COL_V + head * DK : COL_V + (head + 1) * DK]
                values[chunk, head] = value * beta_col

    def prepare_two(pair, unused):
        prepare(2 * pair)
        prepare(2 * pair + 1)
        return unused

    lax.fori_loop(0, CHUNKS // 2, prepare_two, 0)

    opening = jnp.where(scal[2] > 0, 0.0, 1.0)
    identity = jnp.where(row == col, opening, 0.0)
    for key in range(KEYS):
        for half in range(2):
            state[key, :, 2 * half * DK : (2 * half + 1) * DK] = jnp.zeros((DK, DK), F32)
            state[key, :, (2 * half + 1) * DK : (2 * half + 2) * DK] = identity

    def advance(chunk, unused):
        reset = jnp.logical_and(chunk == CHUNKS // 2, scal[3] > 0)
        keep = jnp.where(reset, 0.0, 1.0)
        beta = betas[chunk]
        log = logs[chunk]
        growth = jnp.exp(log)
        last = log[ROWS - 1 : ROWS, :]
        shrink = jnp.exp(last - log)
        whole = jnp.exp(last)
        for key in range(KEYS):
            held = state[key] * keep
            held_low = held.astype(BF16)
            xs[chunk, key] = held_low
            seen = dot(khat[chunk, key], held_low)
            updates = []
            scales = []
            for half in range(2):
                head = 2 * key + half
                at = HEADS + head
                factor = beta[:, head : head + 1] * growth[:, at : at + 1]
                part = seen[:, 2 * half * DK : (2 * half + 2) * DK] * factor
                wanted = jnp.concatenate([values[chunk, head] - part[:, :DK], -part[:, DK:]], axis=1)
                solved = wanted + dot(rest[chunk, head], wanted.astype(BF16))
                vs[chunk, head] = solved.astype(BF16)
                updates.append((solved * shrink[:, at : at + 1]).astype(BF16))
                scales.append(jnp.broadcast_to(whole[:, at : at + 1], (1, 2 * DK)))
            scale = jnp.concatenate(scales, axis=1)
            state[key] = held * scale + dot(kturn[chunk, key], jnp.concatenate(updates, axis=1))
        return unused

    lax.fori_loop(0, CHUNKS, advance, 0)
    for key in range(KEYS):
        for half in range(2):
            xend[2 * key + half] = state[key, :, 2 * half * DK : (2 * half + 2) * DK].astype(BF16)


def state_call(scal, pieces, tail, taps, decay, bias):
    vmem = pl.BlockSpec(memory_space=pltpu.VMEM)
    hbm = pl.BlockSpec(memory_space=pl.ANY)
    return pl.pallas_call(
        state_kernel,
        out_shape=(
            jax.ShapeDtypeStruct((HEADS, DK, 2 * DK), BF16),
            jax.ShapeDtypeStruct((CHUNKS, KEYS, DK, 4 * DK), BF16),
            jax.ShapeDtypeStruct((CHUNKS, HEADS, ROWS, 2 * DK), BF16),
            jax.ShapeDtypeStruct((CHUNKS, KEYS, ROWS, DK), BF16),
            jax.ShapeDtypeStruct((CHUNKS, ROWS, 128), F32),
        ),
        in_specs=[pl.BlockSpec(memory_space=pltpu.SMEM), hbm, hbm, hbm] + [vmem] * 4,
        out_specs=[vmem] * 5,
        scratch_shapes=[
            pltpu.VMEM((LEAD + CHUNKS * ROWS, COL_Z), BF16),
            pltpu.VMEM((CHUNKS, HEADS, ROWS, ROWS), BF16),
            pltpu.VMEM((CHUNKS, KEYS, DK, ROWS), BF16),
            pltpu.VMEM((CHUNKS, HEADS, ROWS, DK), F32),
            pltpu.VMEM((CHUNKS, ROWS, 128), F32),
            pltpu.VMEM((KEYS, DK, 4 * DK), F32),
            pltpu.SemaphoreType.DMA((CHUNKS,)),
        ],
        compiler_params=pltpu.CompilerParams(vmem_limit_bytes=40 * 1024 * 1024),
        cost_estimate=pl.CostEstimate(flops=6_000_000_000, bytes_accessed=20_000_000, transcendentals=0),
        name="state",
    )(scal, *pieces, tail, taps, decay, bias)


def read_kernel(
    scal, piece_a, piece_b, piece_c, tail, taps, xs, vs, khat, logs, out, raw, sems,
):
    raw[0:LEAD, :] = tail[...]
    fetch_rows(scal, (piece_a, piece_b, piece_c), raw, sems, COL_Q, COL_BA)
    inclusive = iota2(0) >= iota2(1)

    def one(chunk, unused):
        mixed = mixed_rows(raw, chunk, 0, COL_BA - COL_Q, taps, is_reset(scal, chunk))
        unit = unit_heads(mixed)
        log = logs[chunk]
        log_turned = log.T
        growth = jnp.exp(log)
        steps = lax.rem(chunk // NC - scal[0] + NY, NY)
        other = jnp.bitwise_xor(lax.rem(chunk, NC), scal[1])
        for key in range(KEYS):
            query = (unit[key] * DK ** (-0.5)).astype(BF16)
            seen = dot(query, xs[chunk, key])
            products = dot(query, khat[chunk, key], ((1,), (1,)))
            for half in range(2):
                head = 2 * key + half
                at = HEADS + head
                spread = log[:, at : at + 1] - log_turned[at : at + 1, :]
                scores = jnp.where(inclusive, products * jnp.exp(jnp.minimum(spread, 0.0)), 0.0)
                found = seen[:, 2 * half * DK : (2 * half + 2) * DK] * growth[:, at : at + 1]
                found = found + dot(scores.astype(BF16), vs[chunk, head])
                out[other, steps, head] = found.astype(BF16)
        return unused

    lax.fori_loop(0, CHUNKS, one, 0)


def read_call(scal, pieces, tail, taps, xs, vs, khat, logs):
    vmem = pl.BlockSpec(memory_space=pltpu.VMEM)
    hbm = pl.BlockSpec(memory_space=pl.ANY)
    return pl.pallas_call(
        read_kernel,
        out_shape=jax.ShapeDtypeStruct((NC, NY, HEADS, ROWS, 2 * DK), BF16),
        in_specs=[pl.BlockSpec(memory_space=pltpu.SMEM), hbm, hbm, hbm] + [vmem] * 6,
        out_specs=vmem,
        scratch_shapes=[
            pltpu.VMEM((LEAD + CHUNKS * ROWS, COL_BA - COL_Q), BF16),
            pltpu.SemaphoreType.DMA((CHUNKS,)),
        ],
        compiler_params=pltpu.CompilerParams(vmem_limit_bytes=40 * 1024 * 1024),
        cost_estimate=pl.CostEstimate(flops=3_000_000_000, bytes_accessed=20_000_000, transcendentals=0),
        name="read",
    )(scal, *pieces, tail, taps, xs, vs, khat, logs)


def after(late, early):
    moved = dot(late[:, DK:], early)
    if early.shape[1] == DK:
        return moved + late[:, :DK].astype(F32)
    return jnp.concatenate([moved[:, :DK] + late[:, :DK].astype(F32), moved[:, DK:]], axis=1)


def row_kernel(parts, leads):
    held = parts[0]
    leads[0] = held
    for place in range(1, NX):
        held = after(parts[place], held).astype(BF16)
        leads[place] = held


def pair_kernel(near, far, both):
    both[...] = after(near[...], far[...]).astype(BF16)


def open_kernel(pair, far, leads, out):
    opening = after(pair[...], far[...]).astype(BF16)
    out[0] = opening
    for place in range(1, NX):
        out[place] = after(leads[place - 1], opening).astype(BF16)


def small_call(kernel, out_shape, *args):
    return pl.pallas_call(
        kernel,
        out_shape=jax.ShapeDtypeStruct(out_shape, BF16),
        cost_estimate=pl.CostEstimate(flops=100_000_000, bytes_accessed=1_000_000, transcendentals=0),
        name="link",
    )(*args)


def out_kernel(other, scal, found, gates, opening, gain, w_out, out):
    steps = pl.program_id(0)
    row = lax.rem(scal[0] + steps, NY)
    core = scal[1] if other == 0 else 1 - scal[1]
    chunk = row * NC + core
    first = lax.rem(chunk, STRETCH // ROWS) * ROWS
    fill = jnp.where(chunk < CHUNKS // 2, scal[4], scal[5])
    within = lax.broadcasted_iota(jnp.int32, (ROWS, 1), 0) + first
    kept = within < fill
    parts = []
    for head in range(HEADS):
        both = found[head]
        value = both[:, :DK].astype(F32) + dot(both[:, DK:], opening[head])
        value = jnp.where(kept, value, 0.0)
        gate = gates[:, head * DK : (head + 1) * DK].astype(F32)
        spread = jnp.mean(value * value, axis=-1, keepdims=True)
        parts.append((value * lax.rsqrt(spread + EPSILON) * gain[...] * silu(gate)).astype(BF16))
    out[...] = dot(jnp.concatenate(parts, axis=1), w_out[...]).astype(BF16)


def out_call(other, scal, found, gates, opening, gain, w_out):
    width = w_out.shape[1]
    return pl.pallas_call(
        lambda *refs: out_kernel(other, *refs),
        grid=(NY,),
        out_shape=jax.ShapeDtypeStruct((NY, ROWS, width), BF16),
        in_specs=[
            pl.BlockSpec(memory_space=pltpu.SMEM),
            pl.BlockSpec((None, None, HEADS, ROWS, 2 * DK), lambda i: (other, i, 0, 0, 0)),
            pl.BlockSpec((None, ROWS, HEADS * DK), lambda i: (i, 0, 0)),
            pl.BlockSpec((HEADS, DK, DK), lambda i: (0, 0, 0)),
            pl.BlockSpec((1, DK), lambda i: (0, 0)),
            pl.BlockSpec((HEADS * DK, width), lambda i: (0, 0)),
        ],
        out_specs=pl.BlockSpec((None, ROWS, width), lambda i: (i, 0, 0)),
        compiler_params=pltpu.CompilerParams(vmem_limit_bytes=40 * 1024 * 1024),
        cost_estimate=pl.CostEstimate(flops=1_200_000_000, bytes_accessed=6_000_000, transcendentals=0),
        name="out",
    )(scal, found, gates, opening, gain, w_out)


def per_device(
    tokens,
    stretch_prompt,
    last_fill,
    ln1_gain,
    w_qk,
    w_vz,
    w_ba,
    conv_qk,
    conv_value,
    decay_log,
    dt_bias,
    norm_gain,
    w_out,
    ln2_gain,
    w_sgate,
    shared_weights,
):
    width = tokens.shape[1]
    place_y = lax.axis_index("y")
    place_core = lax.axis_index("core")
    device = lax.axis_index("z") * NX + lax.axis_index("x")
    normed = scaled_rows(tokens, ln1_gain).astype(BF16)

    below = turn(normed, "y", 1, NY)
    above = turn(normed, "y", -1, NY)
    beside = turn(normed, "core", 1, NC)
    across_up = turn(below[: ROWS // 2], "y", 1, NY)
    across_down = turn(above[ROWS // 2 :], "y", -1, NY)
    middle = jnp.concatenate([above, below], axis=0)
    middle_beside = turn(middle, "core", 1, NC)
    across = jnp.concatenate([across_up, across_down], axis=0)
    across_beside = turn(across, "core", 1, NC)

    weight = jnp.concatenate(
        [
            w_qk[:, 1, :],
            w_vz[:, 0, :],
            w_qk[:, 0, :],
            w_ba.reshape(width, 2 * HEADS),
            jnp.zeros((width, COL_Z - COL_BA - 2 * HEADS), BF16),
            w_vz[:, 1, :],
        ],
        axis=1,
    )

    def project(rows):
        return jnp.dot(rows, weight, preferred_element_type=F32).astype(BF16)

    pieces = (
        project(jnp.concatenate([normed, beside], axis=0)),
        project(jnp.concatenate([middle, middle_beside], axis=0)),
        project(jnp.concatenate([across, across_beside], axis=0)),
    )

    ends = [None] * (NY * NC)
    for (steps, other), (piece, block) in PLACES.items():
        ends[steps * NC + other] = pieces[piece][(block + 1) * ROWS - LEAD : (block + 1) * ROWS, :COL_BA]
    last_place = lax.rem(NY - 1 - place_y + NY, NY) * NC + (NC - 1 - place_core)
    tail = push(lax.dynamic_index_in_dim(jnp.stack(ends), last_place, 0, False), ("z", "x"), 1, NZ * NX)

    first_slot = device * 2
    before = jnp.concatenate([jnp.full((1,), -1, jnp.int32), stretch_prompt])
    later = jnp.concatenate([stretch_prompt, jnp.full((1,), -1, jnp.int32)])
    current = lax.dynamic_slice_in_dim(stretch_prompt, first_slot, 2)
    starts = current != lax.dynamic_slice_in_dim(before, first_slot, 2)
    finishes = current != lax.dynamic_slice_in_dim(later, first_slot + 1, 2)
    fill = jnp.where(finishes, lax.dynamic_slice_in_dim(last_fill, first_slot, 2), STRETCH)
    scal = jnp.concatenate(
        [jnp.stack([place_y, place_core]).astype(jnp.int32), starts.astype(jnp.int32), fill]
    )

    taps_qk = conv_qk.astype(F32)
    taps_kv = jnp.concatenate([taps_qk[:, 1, :], conv_value.astype(F32)], axis=1)
    pad = ((HEADS, 128 - 2 * HEADS),)
    decay = jnp.pad(decay_log, pad)[None, :]
    bias = jnp.pad(dt_bias, pad)[None, :]
    tail_all = jnp.pad(tail, ((0, 0), (0, COL_Z - COL_BA)))
    xend, xs, vs, khat, logs = state_call(scal, pieces, tail_all, taps_kv, decay, bias)

    parts = lax.all_to_all(xend, "x", 0, 0, tiled=True)
    leads = small_call(row_kernel, (NX, DK, 2 * DK), parts)
    near = push(leads[NX - 1], "z", 1, NZ)
    far = push(leads[NX - 1], "z", 2, NZ)
    both = small_call(pair_kernel, (DK, 2 * DK), near, far)
    farther = push(both[:, :DK], "z", 2, NZ)
    openings = small_call(open_kernel, (NX, DK, DK), both, farther, leads)
    opening = lax.all_to_all(openings, "x", 0, 0, tiled=True)

    found = read_call(scal, pieces, tail[:, COL_Q:], taps_qk[:, 0, :], xs, vs, khat, logs)

    def gates_of(other):
        picked = []
        for steps in range(NY):
            piece, block = PLACES[(steps, other)]
            picked.append(pieces[piece][block * ROWS : (block + 1) * ROWS, COL_Z:])
        return jnp.stack(picked)

    gain = norm_gain.astype(F32)[None, :]
    given = out_call(1, scal, found, gates_of(1), opening, gain, w_out)
    received = turn(given, "core", 1, NC)
    own = out_call(0, scal, found, gates_of(0), opening, gain, w_out)

    def add(left, right):
        return (left.astype(F32) + right.astype(F32)).astype(BF16)

    summed = add(own, received)
    half = width // 2
    pass_up = turn(summed[2, :, :half], "y", 1, NY)
    pass_down = turn(summed[2, :, half:], "y", -1, NY)
    up = jnp.concatenate([add(summed[1, :, :half], pass_up), summed[1, :, half:]], axis=1)
    down = jnp.concatenate([summed[3, :, :half], add(summed[3, :, half:], pass_down)], axis=1)
    got_up = turn(up, "y", 1, NY)
    got_down = turn(down, "y", -1, NY)
    attention_out = (summed[0].astype(F32) + got_up.astype(F32) + got_down.astype(F32)).astype(BF16)

    residual = add(tokens, attention_out)
    normed_two = scaled_rows(residual, ln2_gain).astype(BF16)
    expert_gate = jax.nn.sigmoid(jnp.dot(normed_two, w_sgate, preferred_element_type=F32))
    gathered = lax.all_gather(shared_weights, ("y", "core"), axis=1, tiled=True)
    gate_part = jnp.einsum("rd,fd->rf", normed_two, gathered[0], preferred_element_type=F32)
    up_part = jnp.einsum("rd,fd->rf", normed_two, gathered[1], preferred_element_type=F32)
    hidden = (jax.nn.silu(gate_part) * up_part).astype(BF16)
    expert = jnp.dot(hidden, gathered[2], preferred_element_type=F32)
    layer_out = (residual.astype(F32) + expert_gate[:, None] * expert).astype(BF16)
    return (attention_out, layer_out)


def solution(mesh):
    fine = Mesh(mesh.devices.reshape(NZ, NX, NY, NC), ("z", "x", "y", "core"))
    rows = P(("z", "x", "y", "core"), None)
    head = ("y", "core")
    return jax.shard_map(
        per_device,
        mesh=fine,
        in_specs=(
            rows,
            P(),
            P(),
            P(),
            P(None, None, head),
            P(None, None, head),
            P(None, None, head),
            P(None, None, head),
            P(None, head),
            P(head),
            P(head),
            P(),
            P(head, None),
            P(),
            P(),
            P(None, head, None),
        ),
        out_specs=(rows, rows),
        check_vma=False,
    )
```

time: 751 us -> 255 us (0.34)
  waiting for transfers between devices: 268 us -> 23.7 us
  matrix products: 197 us -> 21.5 us
  starting transfers between devices: 178 us -> 44.9 us
  Pallas kernels: 0 us -> 76.3 us
  other arithmetic: 24.2 us -> 9.24 us
    dot_general x85 -> x6, matrix products: 197 us -> 21.5 us  [the longest x3 14.5 us: project(): return jnp.dot(rows, weight, preferred_element_type=F32).astype(BF16)]
    ppermute x33 -> x16, starting transfers between devices: 178 us -> 36.8 us  [the longest x12 19 us: turn(): lax.ppermute(value, axis, [(i, (i + steps) % count) for i in range(count)])]
    reduce_scatter x1 -> x0, waiting for transfers between devices: 120 us -> none  [per_device(): lax.psum_scatter(jnp.dot(gated, w_out, preferred_element_type=jnp.float32...]
    pallas_call x0 -> x7, Pallas kernels: none -> 76.3 us  [the longest x1 57.9 us: state_call(): pl.pallas_call(state_kernel, out_shape=(jax.ShapeDtypeStruct((HEADS, DK,...]
    all_gather x2 -> x1, waiting for transfers between devices: 73.2 us -> 0.01 us  [per_device(): gathered = lax.all_gather(shared_weights, ('y', 'core'), axis=1, tiled=True)]
    ppermute x33 -> x16, waiting for transfers between devices: 74.1 us -> 18.9 us  [the longest x12 17.1 us: turn(): lax.ppermute(value, axis, [(i, (i + steps) % count) for i in range(count)])]
    reshape x8 -> x2, local copies, waits for them, and re-layouts: 16.8 us -> 1.02 us  [per_device(): w_ba.reshape(width, 2 * HEADS)]
    slice x9 -> x6, local copies, waits for them, and re-layouts: 2.95 us -> 17.9 us  [the longest x1 10.3 us: per_device(): w_vz[:, 1, :]]
  transfers between devices with their start and end apart: 36 -> 19, of which waited for: 34 -> 7; matrix products, arithmetic and copies ran while one was open for 2% -> 25% of each run, Pallas kernels for 0% -> 30%
where the time goes in v1:
time: 255 us; the launch traced here: 250 us
  Pallas kernels  76.3 us (30%)
  local copies, waits for them, and re-layouts  60.1 us (24%)
  starting transfers between devices  44.9 us (18%)
  waiting for transfers between devices  23.7 us (9%)
  matrix products  21.5 us (8%)
  between operations  14.6 us (6%)
  other arithmetic  9.24 us (4%)
    pallas_call x1, Pallas kernels, state_call(): pl.pallas_call(state_kernel, out_shape=(jax.ShapeDtypeStruct((HEADS, DK,...  57.9 us
    ppermute x12, starting transfers between devices, turn(): lax.ppermute(value, axis, [(i, (i + steps) % count) for i in range(count)])  19 us
    ppermute x4, starting transfers between devices, push(): lax.ppermute(value, axis, [(i, i + steps) for i in range(count - steps)])  17.8 us
    ppermute x12, waiting for transfers between devices, turn(): lax.ppermute(value, axis, [(i, (i + steps) % count) for i in range(count)])  17.1 us
    unnamed x84, local copies, waits for them, and re-layouts  16.5 us
    dot_general x3, matrix products, project(): return jnp.dot(rows, weight, preferred_element_type=F32).astype(BF16)  14.5 us
    concatenate x1, local copies, waits for them, and re-layouts, per_device(): jnp.concatenate([w_qk[:, 1, :], w_vz[:, 0, :], w_qk[:, 0, :], w_ba.reshap...  10.5 us
    slice x1, local copies, waits for them, and re-layouts, per_device(): w_vz[:, 1, :]  10.3 us
  transfers between devices with their start and end apart: 19, of which 7 were waited for; matrix products, arithmetic and copies ran while one was open for 25% of the time, Pallas kernels for 30%

profile of v1, /device:TPU:1, one launch (start us, length us, event | category | flops | bytes accessed | tf_op | source)
XLA Modules:
  0.0 250.4 jit_solution(17293525783166245040)
XLA Ops:
  11.2 3.2 %collective-permute-start = (bf16[128,2048]{1,0:T(8,128)(2,1)}, bf16[128,2048]{1,0:T(8,128)(2,1)}, u32[]{:S(2)}, u32[]{:S(2)}) collective-permute-start(bf16[128,2048]{1,0:T(8,128)(2,1)} %fusion.17), channel_id=1, source_target_pairs={{0,1},{1,0},{2,3},{3,2},{4,5},{5,4},{6,7},{7,6},{8,9},{9,8},{10,11... | collective-permute-start | bytes 1572872 | tf_op jit(solution)/shard_map/ppermute | solution.py:56
  15.9 10.3 %fusion.66 = (bf16[2048,1,512]{2,1,0:T(2,128)(2,1)}, bf16[2048,1,512]{2,1,0:T(2,128)(2,1)}) fusion(bf16[2048,2,512]{2,1,0:T(2,128)(2,1)} %param.21), kind=kLoop, calls=%fused_computation.124 | loop fusion | bytes 8388608 | tf_op jit(solution)/shard_map/slice | solution.py:413
  26.2 4.2 %fusion.67 = (bf16[2048,1,256]{2,1,0:T(2,128)(2,1)}, bf16[2048,1,256]{2,1,0:T(2,128)(2,1)}) fusion(bf16[2048,2,256]{2,1,0:T(2,128)(2,1)S(1)} %copy-done.15), kind=kLoop, calls=%fused_computation.125 | loop fusion | bytes 4194304 | tf_op jit(solution)/shard_map/slice | solution.py:410
  30.5 6.7 %copy_bitcast_fusion = (bf16[2048,512]{1,0:T(8,128)(2,1)S(1)}, bf16[2048,512]{1,0:T(8,128)(2,1)}) fusion(bf16[2048,1,512]{2,1,0:T(2,128)(2,1)} %get-tuple-element.15, bf16[2048,1,512]{2,1,0:T(2,128)(2,1)} %get-tuple-element.16), kind=kLoop, calls=%fused_computation.17 | loop fusion | bytes 8388608 | tf_op jit(solution)/shard_map/squeeze | solution.py:413
  37.5 3.6 %copy_bitcast_fusion.2 = (bf16[2048,256]{1,0:T(8,128)(2,1)S(1)}, bf16[2048,256]{1,0:T(8,128)(2,1)}) fusion(bf16[2048,1,256]{2,1,0:T(2,128)(2,1)} %get-tuple-element.23, bf16[2048,1,256]{2,1,0:T(2,128)(2,1)} %get-tuple-element.24), kind=kLoop, calls=%fused_computation.47 | loop fusion | bytes 4194304 | tf_op jit(solution)/shard_map/squeeze | solution.py:410
  48.5 10.5 %concatenate.42 = bf16[2048,1664]{1,0:T(8,128)(2,1)} concatenate(bf16[2048,256]{1,0:T(8,128)(2,1)} %get-tuple-element.38, bf16[2048,512]{1,0:T(8,128)(2,1)} %get-tuple-element.40, bf16[2048,256]{1,0:T(8,128)(2,1)S(1)} %get-tuple-element.37, bf16[2048,8]{1,0:T(8,128)(2,1)} %copy.33, bf16[2048,120]{1,0:T(8,128)(2,1)} %broadcast_in_dim.24, bf16[2048,512]{1,0:T(8,128)(2,1)S(1)} %get-tuple-element.39), dimensions={1} | concatenate | bytes 13631488 | tf_op jit(solution)/shard_map/concatenate | solution.py:406
  63.1 5.7 %convolution_convert_fusion.2.piece_a = bf16[256,1664]{1,0:T(8,128)(2,1)S(1)} fusion(bf16[2048,1664]{1,0:T(8,128)(2,1)} %concatenate.42, bf16[128,2048]{1,0:T(8,128)(2,1)} %collective-permute-done, bf16[128,2048]{1,0:T(8,128)(2,1)} %fusion.17), kind=kOutput, calls=%fused_computation.3 | convolution fusion | flops 1747353600 | bytes 8716288 | tf_op jit(solution)/shard_map/dot_general | solution.py:419
  68.9 3.3 %convolution_convert_fusion.1.piece_c = bf16[256,1664]{1,0:T(8,128)(2,1)S(1)} fusion(bf16[2048,1664]{1,0:T(8,128)(2,1)S(1)} %bitcast.129, bf16[128,2048]{1,0:T(8,128)(2,1)S(1)} %collective-permute-done.6, bf16[64,2048]{1,0:T(8,128)(2,1)} %collective-permute-done.5, bf16[64,2048]{1,0:T(8,128)(2,1)} %collective-permute-done.4), kind=kOutput, calls=%fused_computation.2 | convolution fusion | flops 1748402176 | bytes 8716288 | tf_op jit(solution)/shard_map/dot_general | solution.py:419
  72.3 5.5 %convolution_convert_fusion.piece_b = bf16[512,1664]{1,0:T(8,128)(2,1)S(1)} fusion(bf16[2048,1664]{1,0:T(8,128)(2,1)S(1)} %bitcast.129, bf16[256,2048]{1,0:T(8,128)(2,1)S(1)} %collective-permute-done.3, bf16[128,2048]{1,0:T(8,128)(2,1)} %collective-permute-done.2, bf16[128,2048]{1,0:T(8,128)(2,1)} %collective-permute-done.1), kind=kOutput, calls=%fused_computation.1 | convolution fusion | flops 3496804352 | bytes 10616832 | tf_op jit(solution)/shard_map/dot_general | solution.py:419
  81.3 57.9 %state.1 = (bf16[4,128,256]{2,1,0:T(8,128)(2,1)}, bf16[8,2,128,512]{3,2,1,0:T(8,128)(2,1)S(1)}, bf16[8,4,128,256]{3,2,1,0:T(8,128)(2,1)S(1)}, bf16[8,2,128,128]{3,2,1,0:T(8,128)(2,1)S(1)}, f32[8,128,128]{2,1,0:T(8,128)S(1)}) custom-call(s32[6]{0:T(128)S(1)} %pad_add_fusion.2.scal.refs_0_, bf16[256,1664]{1,0:T(8,128)(2,1)S(1)} %convolution_convert_fusion.2.piece_a, ...), custom_call_target="tpu_custom_call" | custom-call | flops 6000000000 | bytes 20000000 | tf_op jit(solution)/shard_map/state/pallas_call | solution.py:220
  142.7 4.5 %all-to-all-start = ((bf16[4,128,256]{2,1,0:T(8,128)(2,1)}), bf16[4,128,256]{2,1,0:T(8,128)(2,1)S(1)}, u32[]{:S(2)}, u32[]{:S(2)}) async-start(bf16[4,128,256]{2,1,0:T(8,128)(2,1)} %get-tuple-element.11), calls=%async_computation | async-start | bytes 524288 | tf_op jit(solution)/shard_map/all_to_all | solution.py:452
  148.0 4.8 %all-to-all-done.parts = bf16[4,128,256]{2,1,0:T(8,128)(2,1)S(1)} async-done(((bf16[4,128,256]{2,1,0:T(8,128)(2,1)}), bf16[4,128,256]{2,1,0:T(8,128)(2,1)S(1)}, u32[]{:S(2)}, u32[]{:S(2)}) %all-to-all-start) | async-done | bytes 262176 | tf_op jit(solution)/shard_map/all_to_all | solution.py:452
  156.4 5.0 %collective-permute-start.8 = (bf16[128,256]{1,0:T(8,128)(2,1)S(1)}, bf16[128,256]{1,0:T(8,128)(2,1)S(1)}, u32[]{:S(2)}, u32[]{:S(2)}) collective-permute-start(bf16[128,256]{1,0:T(8,128)(2,1)S(1)} %slice_bitcast_fusion.27), channel_id=1, source_target_pairs={{0,32},{32,64},{64,96},{96,128},{128,160},{160,192},{192,224},{1,3... | collective-permute-start | bytes 196616 | tf_op jit(solution)/shard_map/ppermute | solution.py:60
  161.4 4.7 %collective-permute-start.9 = (bf16[128,256]{1,0:T(8,128)(2,1)S(1)}, bf16[128,256]{1,0:T(8,128)(2,1)S(1)}, u32[]{:S(2)}, u32[]{:S(2)}) collective-permute-start(bf16[128,256]{1,0:T(8,128)(2,1)S(1)} %slice_bitcast_fusion.27), channel_id=1, source_target_pairs={{0,64},{32,96},{64,128},{96,160},{128,192},{160,224},{1,65},{33,97... | collective-permute-start | bytes 196616 | tf_op jit(solution)/shard_map/ppermute | solution.py:60
  170.5 5.6 %collective-permute-start.10 = (bf16[128,128]{1,0:T(8,128)(2,1)S(1)}, bf16[128,128]{1,0:T(8,128)(2,1)S(1)}, u32[]{:S(2)}, u32[]{:S(2)}) collective-permute-start(bf16[128,128]{1,0:T(8,128)(2,1)S(1)} %slice.167), channel_id=1, source_target_pairs={{0,64},{32,96},{64,128},{96,160},{128,192},{160,224},{1,65},{33,97... | collective-permute-start | bytes 98312 | tf_op jit(solution)/shard_map/ppermute | solution.py:60
  179.7 3.5 %all-to-all-start.1 = ((bf16[4,128,128]{2,1,0:T(8,128)(2,1)}), bf16[4,128,128]{2,1,0:T(8,128)(2,1)S(1)}, u32[]{:S(2)}, u32[]{:S(2)}) async-start(bf16[4,128,128]{2,1,0:T(8,128)(2,1)} %link.5), calls=%async_computation.1 | async-start | bytes 262144 | tf_op jit(solution)/shard_map/all_to_all | solution.py:459
  191.2 6.1 %read.1.refs_1_ = bf16[2,4,4,128,256]{4,3,2,1,0:T(8,128)(2,1)S(1)} custom-call(s32[6]{0:T(128)S(1)} %pad_add_fusion.2.scal.refs_0_, bf16[256,1664]{1,0:T(8,128)(2,1)S(1)} %copy-done.6, bf16[512,1664]{1,0:T(8,128)(2,1)S(1)} %copy-done.4, bf16[256,1664]{1,0:T(8,128)(2,1)S(1)} %copy-done.8, bf16[16,256]{1,0:T(8,128)(2,1)S(1)} %slice.159.tail, ...), custom_call_target="tpu_custom_call" | custom-call | flops 3000000000 | bytes 20000000 | tf_op jit(solution)/shard_map/read/pallas_call | solution.py:281
  200.3 3.3 %out.3 = bf16[4,128,2048]{2,1,0:T(8,128)(2,1)S(1)} custom-call(s32[6]{0:T(128)S(1)} %pad_add_fusion.2.scal.refs_0_, bf16[2,4,4,128,256]{4,3,2,1,0:T(8,128)(2,1)S(1)} %copy-done.2, bf16[4,128,512]{2,1,0:T(8,128)(2,1)S(1)} %pad_maximum_fusion.3.refs_2_, bf16[4,128,128]{2,1,0:T(8,128)(2,1)S(1)} %all-to-all-done.1.refs_3_, ...), custom_call_target="tpu_custom_call" | custom-call | flops 1200000000 | bytes 6000000 | tf_op jit(solution)/shard_map/out/pallas_call | solution.py:353
  203.6 4.4 %collective-permute-start.11 = (bf16[4,128,2048]{2,1,0:T(8,128)(2,1)S(1)}, bf16[4,128,2048]{2,1,0:T(8,128)(2,1)S(1)}, u32[]{:S(2)}, u32[]{:S(2)}) collective-permute-start(bf16[4,128,2048]{2,1,0:T(8,128)(2,1)S(1)} %out.3), channel_id=1, source_target_pairs={{0,1},{1,0},{2,3},{3,2},{4,5},{5,4},{6,7},{7,6},{8,9},{9,8},{10,11... | collective-permute-start | bytes 6291464 | tf_op jit(solution)/shard_map/ppermute | solution.py:56
  208.1 3.3 %out.2 = bf16[4,128,2048]{2,1,0:T(8,128)(2,1)S(1)} custom-call(s32[6]{0:T(128)S(1)} %pad_add_fusion.2.scal.refs_0_, bf16[2,4,4,128,256]{4,3,2,1,0:T(8,128)(2,1)S(1)} %copy-done.2, bf16[4,128,512]{2,1,0:T(8,128)(2,1)S(1)} %pad_maximum_fusion.2.refs_2_, bf16[4,128,128]{2,1,0:T(8,128)(2,1)S(1)} %all-to-all-done.1.refs_3_, ...), custom_call_target="tpu_custom_call" | custom-call | flops 1200000000 | bytes 6000000 | tf_op jit(solution)/shard_map/out/pallas_call | solution.py:353
  215.5 6.1 %collective-permute-done.12 = bf16[128,1024]{1,0:T(8,128)(2,1)S(1)} collective-permute-done((bf16[128,1024]{1,0:T(8,128)(2,1)S(1)}, bf16[128,1024]{1,0:T(8,128)(2,1)S(1)}, u32[]{:S(2)}, u32[]{:S(2)}) %collective-permute-start.12) | collective-permute-done | bytes 262176 | tf_op jit(solution)/shard_map/ppermute | solution.py:56
  221.9 2.7 %collective-permute-start.15 = (bf16[128,2048]{1,0:T(8,128)(2,1)S(1)}, bf16[128,2048]{1,0:T(8,128)(2,1)S(1)}, u32[]{:S(2)}, u32[]{:S(2)}) collective-permute-start(bf16[128,2048]{1,0:T(8,128)(2,1)S(1)} %pad_maximum_fusion.5), channel_id=1, source_target_pairs={{0,6},{2,0},{4,2},{6,4},{1,7},{3,1},{5,3},{7,5},{8,14},{10,8},{12,... | collective-permute-start | bytes 1572872 | tf_op jit(solution)/shard_map/ppermute | solution.py:56
  224.7 10.6 %collective-permute-done.13 = bf16[128,2048]{1,0:T(8,128)(2,1)S(1)} collective-permute-done((bf16[128,2048]{1,0:T(8,128)(2,1)S(1)}, bf16[128,2048]{1,0:T(8,128)(2,1)S(1)}, u32[]{:S(2)}, u32[]{:S(2)}) %collective-permute-start.13) | collective-permute-done | bytes 524320 | tf_op jit(solution)/shard_map/ppermute | solution.py:56
  239.3 4.3 %fusion.1 = bf16[128,2048]{1,0:T(8,128)(2,1)} fusion(bf16[3,512,2048]{2,1,0:T(8,128)(2,1)} %all-gather.2.cloned.1.call-done, bf16[128,2048]{1,0:T(8,128)(2,1)S(1)} %get-tuple-element.13, f32[128]{0:T(128)S(1)} %fusion.14, f32[2048]{0:T(1024)S(1)} %convert_element_type.132, f32[128]{0:T(128)S(1)} %add_rsqrt_fusion, f32[128,512]{1,0:T(8,128)S(1)} %fusion.3), kind=kOutput, calls=%fused_computation.6 | convolution fusion | flops 539361280 | bytes 6038528 | tf_op jit(solution)/shard_map/dot_general | solution.py:495
  (158 shorter events, 56.0 us)
Async XLA Ops:
  7.2 229.7 %all-gather.2.cloned.1.call-start = ((), (), s32[]{:S(2)}) async-start(), calls=%async_computation.2 | async-start | bytes 7077888 | tf_op jit(solution)/shard_map/all_gather | solution.py:491
  11.2 52.0 %collective-permute-start = (bf16[128,2048]{1,0:T(8,128)(2,1)}, bf16[128,2048]{1,0:T(8,128)(2,1)}, u32[]{:S(2)}, u32[]{:S(2)}) collective-permute-start(bf16[128,2048]{1,0:T(8,128)(2,1)} %fusion.17), channel_id=1, source_target_pairs={{0,1},{1,0},{2,3},{3,2},{4,5},{5,4},{6,7},{7,6},{8,9},{9,8},{10,11... | collective-permute-start | bytes 1572872 | tf_op jit(solution)/shard_map/ppermute | solution.py:56
  14.4 28.1 %collective-permute-start.1 = (bf16[128,2048]{1,0:T(8,128)(2,1)}, bf16[128,2048]{1,0:T(8,128)(2,1)}, u32[]{:S(2)}, u32[]{:S(2)}) collective-permute-start(bf16[128,2048]{1,0:T(8,128)(2,1)} %fusion.17), channel_id=1, source_target_pairs={{0,6},{2,0},{4,2},{6,4},{1,7},{3,1},{5,3},{7,5},{8,14},{10,8},{12,... | collective-permute-start | bytes 1572872 | tf_op jit(solution)/shard_map/ppermute | solution.py:56
  15.4 25.7 %collective-permute-start.2 = (bf16[128,2048]{1,0:T(8,128)(2,1)}, bf16[128,2048]{1,0:T(8,128)(2,1)}, u32[]{:S(2)}, u32[]{:S(2)}) collective-permute-start(bf16[128,2048]{1,0:T(8,128)(2,1)} %fusion.17), channel_id=1, source_target_pairs={{0,2},{2,4},{4,6},{6,0},{1,3},{3,5},{5,7},{7,1},{8,10},{10,12},{12... | collective-permute-start | bytes 1572872 | tf_op jit(solution)/shard_map/ppermute | solution.py:56
  42.1 19.4 %collective-permute-start.4 = (bf16[64,2048]{1,0:T(8,128)(2,1)S(1)}, bf16[64,2048]{1,0:T(8,128)(2,1)}, u32[]{:S(2)}, u32[]{:S(2)}) collective-permute-start(bf16[64,2048]{1,0:T(8,128)(2,1)S(1)} %slice.149), channel_id=1, source_target_pairs={{0,2},{2,4},{4,6},{6,0},{1,3},{3,5},{5,7},{7,1},{8,10},{10,12},{12... | collective-permute-start | bytes 786440 | tf_op jit(solution)/shard_map/ppermute | solution.py:56
  44.2 17.4 %collective-permute-start.5 = (bf16[64,2048]{1,0:T(8,128)(2,1)}, bf16[64,2048]{1,0:T(8,128)(2,1)}, u32[]{:S(2)}, u32[]{:S(2)}) collective-permute-start(bf16[64,2048]{1,0:T(8,128)(2,1)} %slice.150), channel_id=1, source_target_pairs={{0,6},{2,0},{4,2},{6,4},{1,7},{3,1},{5,3},{7,5},{8,14},{10,8},{12,... | collective-permute-start | bytes 786440 | tf_op jit(solution)/shard_map/ppermute | solution.py:56
  60.2 12.0 %collective-permute-start.3 = (bf16[256,2048]{1,0:T(8,128)(2,1)S(1)}, bf16[256,2048]{1,0:T(8,128)(2,1)S(1)}, u32[]{:S(2)}, u32[]{:S(2)}) collective-permute-start(bf16[256,2048]{1,0:T(8,128)(2,1)S(1)} %pad_maximum_fusion), channel_id=1, source_target_pairs={{0,1},{1,0},{2,3},{3,2},{4,5},{5,4},{6,7},{7,6},{8,9},{9,8},{10,11... | collective-permute-start | bytes 3145736 | tf_op jit(solution)/shard_map/ppermute | solution.py:56
  62.9 6.0 %collective-permute-start.6 = (bf16[128,2048]{1,0:T(8,128)(2,1)S(1)}, bf16[128,2048]{1,0:T(8,128)(2,1)S(1)}, u32[]{:S(2)}, u32[]{:S(2)}) collective-permute-start(bf16[128,2048]{1,0:T(8,128)(2,1)S(1)} %pad_maximum_fusion.1), channel_id=1, source_target_pairs={{0,1},{1,0},{2,3},{3,2},{4,5},{5,4},{6,7},{7,6},{8,9},{9,8},{10,11... | collective-permute-start | bytes 1572872 | tf_op jit(solution)/shard_map/ppermute | solution.py:56
  72.3 75.0 %copy-start.7 = (bf16[256,1664]{1,0:T(8,128)(2,1)}, bf16[256,1664]{1,0:T(8,128)(2,1)S(1)}, u32[]{:S(2)}) copy-start(bf16[256,1664]{1,0:T(8,128)(2,1)S(1)} %convolution_convert_fusion.1.piece_c) | copy-start | bytes 2555908
  77.7 88.4 %copy-start.3 = (bf16[512,1664]{1,0:T(8,128)(2,1)}, bf16[512,1664]{1,0:T(8,128)(2,1)S(1)}, u32[]{:S(2)}) copy-start(bf16[512,1664]{1,0:T(8,128)(2,1)S(1)} %convolution_convert_fusion.piece_b) | copy-start | bytes 5111812
  77.8 3.5 %collective-permute-start.7 = (bf16[16,1024]{1,0:T(8,128)(2,1)S(1)}, bf16[16,1024]{1,0:T(8,128)(2,1)S(1)}, u32[]{:S(2)}, u32[]{:S(2)}) collective-permute-start(bf16[16,1024]{1,0:T(8,128)(2,1)S(1)} %dynamic-slice_bitcast_fusion), channel_id=1, source_target_pairs={{0,8},{8,16},{16,24},{24,32},{32,40},{40,48},{48,56},{56,64},{64,7... | collective-permute-start | bytes 98312 | tf_op jit(solution)/shard_map/ppermute | solution.py:60
  142.7 10.1 %all-to-all-start = ((bf16[4,128,256]{2,1,0:T(8,128)(2,1)}), bf16[4,128,256]{2,1,0:T(8,128)(2,1)S(1)}, u32[]{:S(2)}, u32[]{:S(2)}) async-start(bf16[4,128,256]{2,1,0:T(8,128)(2,1)} %get-tuple-element.11), calls=%async_computation | async-start | bytes 524288 | tf_op jit(solution)/shard_map/all_to_all | solution.py:452
  148.0 28.2 %copy-start.19 = (bf16[1,128,512]{2,1,0:T(8,128)(2,1)S(1)}, bf16[1,128,512]{2,1,0:T(8,128)(2,1)}, u32[]{:S(2)}) copy-start(bf16[1,128,512]{2,1,0:T(8,128)(2,1)} %get-tuple-element.30) | copy-start | bytes 393220
  148.0 28.2 %copy-start.20 = (bf16[1,128,512]{2,1,0:T(8,128)(2,1)S(1)}, bf16[1,128,512]{2,1,0:T(8,128)(2,1)}, u32[]{:S(2)}) copy-start(bf16[1,128,512]{2,1,0:T(8,128)(2,1)} %get-tuple-element.32) | copy-start | bytes 393220
  156.4 10.5 %collective-permute-start.8 = (bf16[128,256]{1,0:T(8,128)(2,1)S(1)}, bf16[128,256]{1,0:T(8,128)(2,1)S(1)}, u32[]{:S(2)}, u32[]{:S(2)}) collective-permute-start(bf16[128,256]{1,0:T(8,128)(2,1)S(1)} %slice_bitcast_fusion.27), channel_id=1, source_target_pairs={{0,32},{32,64},{64,96},{96,128},{128,160},{160,192},{192,224},{1,3... | collective-permute-start | bytes 196616 | tf_op jit(solution)/shard_map/ppermute | solution.py:60
  161.4 6.0 %collective-permute-start.9 = (bf16[128,256]{1,0:T(8,128)(2,1)S(1)}, bf16[128,256]{1,0:T(8,128)(2,1)S(1)}, u32[]{:S(2)}, u32[]{:S(2)}) collective-permute-start(bf16[128,256]{1,0:T(8,128)(2,1)S(1)} %slice_bitcast_fusion.27), channel_id=1, source_target_pairs={{0,64},{32,96},{64,128},{96,160},{128,192},{160,224},{1,65},{33,97... | collective-permute-start | bytes 196616 | tf_op jit(solution)/shard_map/ppermute | solution.py:60
  170.5 6.6 %collective-permute-start.10 = (bf16[128,128]{1,0:T(8,128)(2,1)S(1)}, bf16[128,128]{1,0:T(8,128)(2,1)S(1)}, u32[]{:S(2)}, u32[]{:S(2)}) collective-permute-start(bf16[128,128]{1,0:T(8,128)(2,1)S(1)} %slice.167), channel_id=1, source_target_pairs={{0,64},{32,96},{64,128},{96,160},{128,192},{160,224},{1,65},{33,97... | collective-permute-start | bytes 98312 | tf_op jit(solution)/shard_map/ppermute | solution.py:60
  179.7 19.0 %all-to-all-start.1 = ((bf16[4,128,128]{2,1,0:T(8,128)(2,1)}), bf16[4,128,128]{2,1,0:T(8,128)(2,1)S(1)}, u32[]{:S(2)}, u32[]{:S(2)}) async-start(bf16[4,128,128]{2,1,0:T(8,128)(2,1)} %link.5), calls=%async_computation.1 | async-start | bytes 262144 | tf_op jit(solution)/shard_map/all_to_all | solution.py:459
  203.6 8.2 %collective-permute-start.11 = (bf16[4,128,2048]{2,1,0:T(8,128)(2,1)S(1)}, bf16[4,128,2048]{2,1,0:T(8,128)(2,1)S(1)}, u32[]{:S(2)}, u32[]{:S(2)}) collective-permute-start(bf16[4,128,2048]{2,1,0:T(8,128)(2,1)S(1)} %out.3), channel_id=1, source_target_pairs={{0,1},{1,0},{2,3},{3,2},{4,5},{5,4},{6,7},{7,6},{8,9},{9,8},{10,11... | collective-permute-start | bytes 6291464 | tf_op jit(solution)/shard_map/ppermute | solution.py:56
  212.7 22.6 %copy-start.16 = (bf16[128,2048]{1,0:T(8,128)(2,1)S(1)}, bf16[128,2048]{1,0:T(8,128)(2,1)}, u32[]{:S(2)}) copy-start(bf16[128,2048]{1,0:T(8,128)(2,1)} %param.16) | copy-start | bytes 1572868
  212.7 8.8 %collective-permute-start.12 = (bf16[128,1024]{1,0:T(8,128)(2,1)S(1)}, bf16[128,1024]{1,0:T(8,128)(2,1)S(1)}, u32[]{:S(2)}, u32[]{:S(2)}) collective-permute-start(bf16[128,1024]{1,0:T(8,128)(2,1)S(1)} %get-tuple-element.19), channel_id=1, source_target_pairs={{0,2},{2,4},{4,6},{6,0},{1,3},{3,5},{5,7},{7,1},{8,10},{10,12},{12... | collective-permute-start | bytes 786440 | tf_op jit(solution)/shard_map/ppermute | solution.py:56
  212.8 8.7 %collective-permute-start.14 = (bf16[128,1024]{1,0:T(8,128)(2,1)S(1)}, bf16[128,1024]{1,0:T(8,128)(2,1)S(1)}, u32[]{:S(2)}, u32[]{:S(2)}) collective-permute-start(bf16[128,1024]{1,0:T(8,128)(2,1)S(1)} %get-tuple-element.20), channel_id=1, source_target_pairs={{0,6},{2,0},{4,2},{6,4},{1,7},{3,1},{5,3},{7,5},{8,14},{10,8},{12,... | collective-permute-start | bytes 786440 | tf_op jit(solution)/shard_map/ppermute | solution.py:56
  221.8 13.5 %collective-permute-start.13 = (bf16[128,2048]{1,0:T(8,128)(2,1)S(1)}, bf16[128,2048]{1,0:T(8,128)(2,1)S(1)}, u32[]{:S(2)}, u32[]{:S(2)}) collective-permute-start(bf16[128,2048]{1,0:T(8,128)(2,1)S(1)} %pad_maximum_fusion.4), channel_id=1, source_target_pairs={{0,2},{2,4},{4,6},{6,0},{1,3},{3,5},{5,7},{7,1},{8,10},{10,12},{12... | collective-permute-start | bytes 1572872 | tf_op jit(solution)/shard_map/ppermute | solution.py:56
  221.9 13.4 %collective-permute-start.15 = (bf16[128,2048]{1,0:T(8,128)(2,1)S(1)}, bf16[128,2048]{1,0:T(8,128)(2,1)S(1)}, u32[]{:S(2)}, u32[]{:S(2)}) collective-permute-start(bf16[128,2048]{1,0:T(8,128)(2,1)S(1)} %pad_maximum_fusion.5), channel_id=1, source_target_pairs={{0,6},{2,0},{4,2},{6,4},{1,7},{3,1},{5,3},{7,5},{8,14},{10,8},{12,... | collective-permute-start | bytes 1572872 | tf_op jit(solution)/shard_map/ppermute | solution.py:56
  (33 other events, 156.6 us)
Sparse Core Ops, SparseCore 0:
  16.0 51.6 all-gather.1

commit v2 on v1

v2 whole, which is shorter than its diff:
```python
import itertools

import jax
import jax.numpy as jnp
from jax import lax
from jax.experimental import pallas as pl
from jax.experimental.pallas import tpu as pltpu
from jax.sharding import Mesh
from jax.sharding import PartitionSpec as P

F32 = jnp.float32
BF16 = jnp.bfloat16
EPSILON = 1e-06
DK = 128
STRETCH = 512
ROWS = 128
CHUNKS = 8
HEADS = 4
KEYS = 2
NZ, NX, NY, NC = 8, 4, 4, 2
LEAD = 16
COL_K = 256
COL_V = 512
COL_BA = 1024
COL_END = 1152
MIB = 1024 * 1024
PLACES = {
    (0, 0): (0, 0),
    (0, 1): (0, 1),
    (1, 0): (1, 0),
    (3, 0): (1, 1),
    (1, 1): (1, 2),
    (3, 1): (1, 3),
    (2, 0): (2, 0),
    (2, 1): (2, 1),
}


def dot(left, right, contract=((1,), (0,))):
    return lax.dot_general(left, right, (contract, ((), ())), preferred_element_type=F32)


def silu(value):
    return value * (0.5 * jnp.tanh(0.5 * value) + 0.5)


def sigmoid(value):
    return 0.5 * jnp.tanh(0.5 * value) + 0.5


def scaled_rows(inputs, scaling):
    widened = inputs.astype(F32)
    spread = jnp.mean(widened * widened, axis=-1, keepdims=True)
    return widened * lax.rsqrt(spread + EPSILON) * scaling.astype(F32)


def hold(value):
    return pltpu.with_memory_space_constraint(value, pltpu.HBM)


def turn(value, axis, steps, count):
    return lax.ppermute(value, axis, [(i, (i + steps) % count) for i in range(count)])


def push(value, axis, steps, count):
    return lax.ppermute(value, axis, [(i, i + steps) for i in range(count - steps)])


def mixed_rows(ref, chunk, first, last, taps, reset):
    start = chunk * ROWS
    rows = ref[pl.ds(start, ROWS + LEAD), first:last].astype(F32)
    if reset is not False:
        rows = jnp.concatenate([jnp.where(reset, 0.0, rows[:LEAD]), rows[LEAD:]], axis=0)
    total = rows[LEAD:] * taps[3:4]
    for offset in (1, 2, 3):
        total = total + rows[LEAD - offset : LEAD - offset + ROWS] * taps[3 - offset : 4 - offset]
    return silu(total)


def unit_heads(value):
    parts = []
    for head in range(value.shape[1] // DK):
        part = value[:, head * DK : (head + 1) * DK]
        parts.append(part * lax.rsqrt(jnp.sum(part * part, axis=-1, keepdims=True) + EPSILON))
    return parts


def fetch_rows(scal, pieces, scratch, sems, first, last, target):
    copies = []
    for (steps, other), (piece, block) in PLACES.items():
        row = lax.rem(scal[0] + steps, NY)
        core = scal[1] if other == 0 else 1 - scal[1]
        chunk = row * NC + core
        start = pl.multiple_of(chunk * ROWS + LEAD, LEAD)
        copy = pltpu.make_async_copy(
            pieces[piece].at[pl.ds(block * ROWS, ROWS), pl.ds(first, last - first)],
            scratch.at[pl.ds(start, ROWS), pl.ds(target, last - first)],
            sems.at[len(copies)],
        )
        copy.start()
        copies.append(copy)
    for copy in copies:
        copy.wait()


def is_reset(scal, chunk):
    if isinstance(chunk, int):
        return scal[2 + chunk * 2 // CHUNKS] > 0 if chunk % (CHUNKS // 2) == 0 else False
    first = jnp.logical_and(chunk == 0, scal[2] > 0)
    second = jnp.logical_and(chunk == CHUNKS // 2, scal[3] > 0)
    return jnp.logical_or(first, second)


def iota2(axis):
    return lax.broadcasted_iota(jnp.int32, (ROWS, ROWS), axis)


def odd_blocks(value, span):
    return jnp.concatenate([value[at : at + span] for at in range(span, ROWS, 2 * span)], axis=0)


def with_even(even, odd, span):
    parts = []
    for place, at in enumerate(range(0, ROWS, 2 * span)):
        block = odd[place * span : (place + 1) * span]
        parts.append(jnp.zeros_like(block) if even is None else even[at : at + span])
        parts.append(block)
    return jnp.concatenate(parts, axis=0)


def inverse_rests(stricts, level):
    rests = [jnp.where(level == 1, -strict, 0.0) for strict in stricts]
    for step in (2, 3):
        lows = [rest.astype(BF16) for rest in rests]
        belows = [jnp.where(level == step, strict, 0.0) for strict in stricts]
        halves = [below + dot(below.astype(BF16), low) for below, low in zip(belows, lows)]
        yield
        rests = [rest - half - dot(low, half.astype(BF16)) for rest, half, low in zip(rests, halves, lows)]
        yield
    for step in (4, 5, 6, 7):
        span = 1 << (step - 1)
        here = odd_blocks(level, span) == step
        lows = [rest.astype(BF16) for rest in rests]
        odds = [odd_blocks(rest, span) for rest in rests]
        belows = [jnp.where(here, odd_blocks(strict, span), 0.0) for strict in stricts]
        halves = [below + dot(below.astype(BF16), low) for below, low in zip(belows, lows)]
        yield
        wides = [with_even(None, half, span).astype(BF16) for half in halves]
        odds = [odd - half - dot(odd.astype(BF16), wide) for odd, half, wide in zip(odds, halves, wides)]
        rests = [with_even(rest, odd, span) for rest, odd in zip(rests, odds)]
        yield
    return rests


def block_levels():
    row, col = iota2(0), iota2(1)
    apart = jnp.where(row > col, jnp.bitwise_xor(row, col), 0)
    level = jnp.zeros((ROWS, ROWS), jnp.int32)
    for step in range(7):
        level = level + (apart >= (1 << step)).astype(jnp.int32)
    return level


def state_kernel(
    scal, piece_a, piece_b, piece_c, tail, taps, decay, bias,
    xend, xs_out, vs_out, khat_out, logs_out,
    raw, rest, kturn, values, betas, state, xs, vs, khat, logs, sems, out_sems,
):
    raw[0:LEAD, 0:COL_BA] = tail[...]
    fetch_rows(scal, (piece_a, piece_b, piece_c), raw, sems, COL_K, COL_END, COL_K)
    row, col = iota2(0), iota2(1)
    strict = row > col
    summing = (row >= col).astype(F32)
    level = block_levels()

    def prepare(chunk):
        reset = is_reset(scal, chunk)
        mixed = mixed_rows(raw, chunk, COL_K, COL_BA, taps, reset)
        start = chunk * ROWS + LEAD
        ba = raw[pl.ds(start, ROWS), COL_BA:COL_END].astype(F32)
        beta = sigmoid(ba)
        inner = ba + bias[...]
        soft = jnp.maximum(inner, 0.0) + jnp.log1p(jnp.exp(-jnp.abs(inner)))
        rate = -jnp.exp(decay[...]) * soft
        log = lax.dot_general(
            summing, rate, (((1,), (0,)), ((), ())),
            precision=lax.Precision.HIGHEST, preferred_element_type=F32,
        )
        log_turned = log.T
        betas[chunk] = beta
        logs[chunk] = log
        unit = unit_heads(mixed[:, : KEYS * DK])
        lowers = []
        for key in range(KEYS):
            key_rows = unit[key].astype(BF16)
            khat[chunk, key] = key_rows
            kturn[chunk, key] = unit[key].T.astype(BF16)
            products = dot(key_rows, key_rows, ((1,), (1,)))
            for half in range(2):
                head = 2 * key + half
                beta_col = beta[:, head : head + 1]
                spread = log[:, HEADS + head : HEADS + head + 1] - log_turned[HEADS + head : HEADS + head + 1, :]
                weight = jnp.exp(jnp.minimum(spread, 0.0))
                lower = jnp.where(strict, products * beta_col * weight, 0.0)
                lowers.append(lower)
                value = mixed[:, (KEYS + head) * DK : (KEYS + head + 1) * DK]
                values[chunk, head] = value * beta_col
        return lowers

    def prepare_all(chunks):
        lowers = []
        for chunk in chunks:
            lowers += prepare(chunk)
            yield
        found = yield from inverse_rests(lowers, level)
        for place, value in enumerate(found):
            rest[chunks[place // HEADS], place % HEADS] = value.astype(BF16)

    opening = jnp.where(scal[2] > 0, 0.0, 1.0)
    identity = jnp.where(row == col, opening, 0.0)
    for key in range(KEYS):
        for half in range(2):
            state[key, :, 2 * half * DK : (2 * half + 1) * DK] = jnp.zeros((DK, DK), F32)
            state[key, :, (2 * half + 1) * DK : (2 * half + 2) * DK] = identity

    def advance(chunk):
        beta = betas[chunk]
        log = logs[chunk]
        growth = jnp.exp(log)
        last = log[ROWS - 1 : ROWS, :]
        shrink = jnp.exp(last - log)
        whole = jnp.exp(last)
        held = [state[key] for key in range(KEYS)]
        if chunk == CHUNKS // 2:
            held = [jnp.where(scal[3] > 0, 0.0, value) for value in held]
        lows = [value.astype(BF16) for value in held]
        for key in range(KEYS):
            xs[chunk, key] = lows[key]
        seen = [dot(khat[chunk, key], lows[key]) for key in range(KEYS)]
        yield
        wanted = []
        for head in range(HEADS):
            at = HEADS + head
            half = head % 2
            factor = beta[:, head : head + 1] * growth[:, at : at + 1]
            part = seen[head // 2][:, 2 * half * DK : (2 * half + 2) * DK] * factor
            wanted.append(jnp.concatenate([values[chunk, head] - part[:, :DK], -part[:, DK:]], axis=1))
        solved = [
            value + dot(rest[chunk, head], value.astype(BF16)) for head, value in enumerate(wanted)
        ]
        yield
        updates = []
        scales = []
        for head in range(HEADS):
            at = HEADS + head
            vs[chunk, head] = solved[head].astype(BF16)
            updates.append((solved[head] * shrink[:, at : at + 1]).astype(BF16))
            scales.append(jnp.broadcast_to(whole[:, at : at + 1], (1, 2 * DK)))
        for key in range(KEYS):
            scale = jnp.concatenate(scales[2 * key : 2 * key + 2], axis=1)
            update = jnp.concatenate(updates[2 * key : 2 * key + 2], axis=1)
            state[key] = held[key] * scale + dot(kturn[chunk, key], update)
        for copy in copies_out(chunk):
            copy.start()
        yield

    def advance_all(chunks):
        for chunk in chunks:
            yield from advance(chunk)

    def copies_out(chunk):
        return [
            pltpu.make_async_copy(held.at[chunk], target.at[chunk], out_sems.at[place, chunk])
            for place, (held, target) in enumerate(((xs, xs_out), (vs, vs_out), (khat, khat_out), (logs, logs_out)))
        ]

    early, late = list(range(CHUNKS // 2)), list(range(CHUNKS // 2, CHUNKS))
    for unused in prepare_all(early):
        pass
    for unused in itertools.zip_longest(prepare_all(late), advance_all(early)):
        pass
    for unused in advance_all(late):
        pass
    for key in range(KEYS):
        for half in range(2):
            xend[2 * key + half] = state[key, :, 2 * half * DK : (2 * half + 2) * DK].astype(BF16)
    for chunk in range(CHUNKS):
        for copy in copies_out(chunk):
            copy.wait()


def state_call(scal, pieces, tail, taps, decay, bias):
    vmem = pl.BlockSpec(memory_space=pltpu.VMEM)
    hbm = pl.BlockSpec(memory_space=pltpu.HBM)
    return pl.pallas_call(
        state_kernel,
        out_shape=(
            jax.ShapeDtypeStruct((HEADS, DK, 2 * DK), BF16),
            pltpu.HBM((CHUNKS, KEYS, DK, 4 * DK), BF16),
            pltpu.HBM((CHUNKS, HEADS, ROWS, 2 * DK), BF16),
            pltpu.HBM((CHUNKS, KEYS, ROWS, DK), BF16),
            pltpu.HBM((CHUNKS, ROWS, 128), F32),
        ),
        in_specs=[pl.BlockSpec(memory_space=pltpu.SMEM), hbm, hbm, hbm] + [vmem] * 4,
        out_specs=[vmem] + [hbm] * 4,
        scratch_shapes=[
            pltpu.VMEM((LEAD + CHUNKS * ROWS, COL_END), BF16),
            pltpu.VMEM((CHUNKS, HEADS, ROWS, ROWS), BF16),
            pltpu.VMEM((CHUNKS, KEYS, DK, ROWS), BF16),
            pltpu.VMEM((CHUNKS, HEADS, ROWS, DK), F32),
            pltpu.VMEM((CHUNKS, ROWS, 128), F32),
            pltpu.VMEM((KEYS, DK, 4 * DK), F32),
            pltpu.VMEM((CHUNKS, KEYS, DK, 4 * DK), BF16),
            pltpu.VMEM((CHUNKS, HEADS, ROWS, 2 * DK), BF16),
            pltpu.VMEM((CHUNKS, KEYS, ROWS, DK), BF16),
            pltpu.VMEM((CHUNKS, ROWS, 128), F32),
            pltpu.SemaphoreType.DMA((CHUNKS,)),
            pltpu.SemaphoreType.DMA((4, CHUNKS)),
        ],
        compiler_params=pltpu.CompilerParams(vmem_limit_bytes=40 * MIB),
        cost_estimate=pl.CostEstimate(flops=6_000_000_000, bytes_accessed=20_000_000, transcendentals=0),
        name="state",
    )(scal, *map(hold, pieces), tail, taps, decay, bias)


def read_kernel(
    scal, piece_a, piece_b, piece_c, tail, taps, xs, vs, khat, logs, out, raw, sems,
):
    step = pl.program_id(0)

    @pl.when(step == 0)
    def _():
        raw[0:LEAD, :] = tail[...]
        fetch_rows(scal, (piece_a, piece_b, piece_c), raw, sems, 0, COL_K, 0)

    inclusive = iota2(0) >= iota2(1)
    queries, weights, growths = [], [], []
    for core in range(NC):
        chunk = NC * step + core
        start = pl.multiple_of(chunk * ROWS, ROWS)
        reset = is_reset(scal, chunk) if core == 0 else False
        mixed = mixed_rows(raw.at[pl.ds(start, ROWS + LEAD)], 0, 0, COL_K, taps, reset)
        queries += [(value * DK ** (-0.5)).astype(BF16) for value in unit_heads(mixed)]
        log = logs[core]
        log_turned = log.T
        growth = jnp.exp(log)
        for head in range(HEADS):
            at = HEADS + head
            growths.append(growth[:, at : at + 1])
            spread = log[:, at : at + 1] - log_turned[at : at + 1, :]
            weights.append(jnp.where(inclusive, jnp.exp(jnp.minimum(spread, 0.0)), 0.0))
    pairs = [(core, key) for core in range(NC) for key in range(KEYS)]
    products = [dot(queries[i], khat[core, key], ((1,), (1,))) for i, (core, key) in enumerate(pairs)]
    seen = [dot(queries[i], xs[core, key]) for i, (core, key) in enumerate(pairs)]
    for core in range(NC):
        other = jnp.bitwise_xor(core, scal[1])
        for head in range(HEADS):
            pair = core * KEYS + head // 2
            half = head % 2
            scores = (products[pair] * weights[core * HEADS + head]).astype(BF16)
            found = seen[pair][:, 2 * half * DK : (2 * half + 2) * DK] * growths[core * HEADS + head]
            out[other, head] = (found + dot(scores, vs[core, head])).astype(BF16)


def read_call(scal, pieces, tail, taps, xs, vs, khat, logs):
    hbm = pl.BlockSpec(memory_space=pltpu.HBM)
    return pl.pallas_call(
        read_kernel,
        out_shape=pltpu.HBM((NC, NY, HEADS, ROWS, 2 * DK), BF16),
        grid_spec=pltpu.PrefetchScalarGridSpec(
            num_scalar_prefetch=1,
            grid=(CHUNKS // NC,),
            in_specs=[
                hbm,
                hbm,
                hbm,
                pl.BlockSpec((LEAD, COL_K), lambda c, scal: (0, 0)),
                pl.BlockSpec((4, COL_K), lambda c, scal: (0, 0)),
                pl.BlockSpec((NC, KEYS, DK, 4 * DK), lambda c, scal: (c, 0, 0, 0)),
                pl.BlockSpec((NC, HEADS, ROWS, 2 * DK), lambda c, scal: (c, 0, 0, 0)),
                pl.BlockSpec((NC, KEYS, ROWS, DK), lambda c, scal: (c, 0, 0, 0)),
                pl.BlockSpec((NC, ROWS, 128), lambda c, scal: (c, 0, 0)),
            ],
            out_specs=pl.BlockSpec(
                (NC, None, HEADS, ROWS, 2 * DK),
                lambda c, scal: (0, lax.rem(c - scal[0] + NY, NY), 0, 0, 0),
            ),
            scratch_shapes=[
                pltpu.VMEM((LEAD + CHUNKS * ROWS, COL_K), BF16),
                pltpu.SemaphoreType.DMA((CHUNKS,)),
            ],
        ),
        compiler_params=pltpu.CompilerParams(vmem_limit_bytes=32 * MIB),
        cost_estimate=pl.CostEstimate(flops=3_000_000_000, bytes_accessed=20_000_000, transcendentals=0),
        name="read",
    )(scal, *map(hold, pieces), tail, taps, hold(xs), hold(vs), hold(khat), hold(logs))


def norm_kernel(tokens, gain, out):
    out[...] = scaled_rows(tokens[...], gain[...][None, :]).astype(BF16)


def norm_call(tokens, gain):
    vmem = pl.BlockSpec(memory_space=pltpu.VMEM)
    return pl.pallas_call(
        norm_kernel,
        out_shape=jax.ShapeDtypeStruct(tokens.shape, BF16),
        in_specs=[vmem, vmem],
        out_specs=vmem,
        cost_estimate=pl.CostEstimate(flops=1_000_000, bytes_accessed=1_000_000, transcendentals=0),
        name="norm",
    )(tokens, gain)


def after(late, early):
    moved = dot(late[:, DK:], early)
    if early.shape[1] == DK:
        return moved + late[:, :DK].astype(F32)
    return jnp.concatenate([moved[:, :DK] + late[:, :DK].astype(F32), moved[:, DK:]], axis=1)


def row_kernel(parts, leads, whole, sums):
    held = parts[0]
    leads[0] = held
    for place in range(1, NX):
        held = after(parts[place], held).astype(BF16)
        if place < NX - 1:
            leads[place] = held
    whole[...] = held
    sums[...] = held[:, :DK]


def row_call(parts):
    vmem = pl.BlockSpec(memory_space=pltpu.VMEM)
    return pl.pallas_call(
        row_kernel,
        out_shape=(
            jax.ShapeDtypeStruct((NX - 1, DK, 2 * DK), BF16),
            jax.ShapeDtypeStruct((DK, 2 * DK), BF16),
            jax.ShapeDtypeStruct((DK, DK), BF16),
        ),
        in_specs=[vmem],
        out_specs=[vmem] * 3,
        cost_estimate=pl.CostEstimate(flops=100_000_000, bytes_accessed=1_000_000, transcendentals=0),
        name="rows",
    )(parts)


def open_kernel(one, two, three, four, leads, out):
    opening = four[...]
    for earlier in (three, two, one):
        opening = after(earlier[...], opening).astype(BF16)
    out[0] = opening
    for place in range(1, NX):
        out[place] = after(leads[place - 1], opening).astype(BF16)


def open_call(earlier, leads):
    vmem = pl.BlockSpec(memory_space=pltpu.VMEM)
    return pl.pallas_call(
        open_kernel,
        out_shape=jax.ShapeDtypeStruct((NX, DK, DK), BF16),
        in_specs=[vmem] * 5,
        out_specs=vmem,
        cost_estimate=pl.CostEstimate(flops=100_000_000, bytes_accessed=1_000_000, transcendentals=0),
        name="open",
    )(*earlier, leads)


def out_kernel(other, scal, found, gates, opening, gain, w_out, out):
    rows = []
    moved = [
        [dot(found[block, head][:, DK:], opening[head]) for head in range(HEADS)]
        for block in range(2)
    ]
    for block in range(2):
        steps = 2 * pl.program_id(0) + block
        core = scal[1] if other == 0 else 1 - scal[1]
        chunk = lax.rem(scal[0] + steps, NY) * NC + core
        first = lax.rem(chunk, STRETCH // ROWS) * ROWS
        fill = jnp.where(chunk < CHUNKS // 2, scal[4], scal[5])
        within = lax.broadcasted_iota(jnp.int32, (ROWS, 1), 0) + first
        kept = within < fill
        parts = []
        for head in range(HEADS):
            value = found[block, head][:, :DK].astype(F32) + moved[block][head]
            value = jnp.where(kept, value, 0.0)
            gate = gates[block, :, head * DK : (head + 1) * DK].astype(F32)
            spread = jnp.mean(value * value, axis=-1, keepdims=True)
            parts.append((value * lax.rsqrt(spread + EPSILON) * gain[...] * silu(gate)).astype(BF16))
        rows.append(jnp.concatenate(parts, axis=1))
    total = dot(jnp.concatenate(rows, axis=0), w_out[...]).astype(BF16)
    out[...] = total.reshape(out.shape)


def out_call(other, scal, found, gates, opening, gain, w_out):
    width = w_out.shape[1]
    return pl.pallas_call(
        lambda *refs: out_kernel(other, *refs),
        grid=(NY // 2,),
        out_shape=jax.ShapeDtypeStruct((NY, ROWS, width), BF16),
        in_specs=[
            pl.BlockSpec(memory_space=pltpu.SMEM),
            pl.BlockSpec((None, 2, HEADS, ROWS, 2 * DK), lambda i: (other, i, 0, 0, 0)),
            pl.BlockSpec((2, ROWS, HEADS * DK), lambda i: (i, 0, 0)),
            pl.BlockSpec((HEADS, DK, DK), lambda i: (0, 0, 0)),
            pl.BlockSpec((1, DK), lambda i: (0, 0)),
            pl.BlockSpec((HEADS * DK, width), lambda i: (0, 0)),
        ],
        out_specs=pl.BlockSpec((2, ROWS, width), lambda i: (i, 0, 0)),
        compiler_params=pltpu.CompilerParams(vmem_limit_bytes=32 * MIB),
        cost_estimate=pl.CostEstimate(flops=1_200_000_000, bytes_accessed=6_000_000, transcendentals=0),
        name="out",
    )(scal, hold(found), hold(gates), opening, gain, hold(w_out))


def expert_kernel(
    summed, got_up, got_down, tokens, gain, w_sgate, shared, attention, layer, weights, sems
):
    copies = [pltpu.make_async_copy(shared.at[i], weights.at[i], sems.at[i]) for i in range(3)]
    for copy in copies:
        copy.start()
    total = summed[...].astype(F32) + got_up[...].astype(F32) + got_down[...].astype(F32)
    total = total.astype(BF16)
    attention[...] = total
    residual = (tokens[...].astype(F32) + total.astype(F32)).astype(BF16)
    normed = scaled_rows(residual, gain[...][None, :]).astype(BF16)
    weighed = normed.astype(F32) * w_sgate[...][None, :].astype(F32)
    gate = sigmoid(jnp.sum(weighed, axis=-1, keepdims=True))
    copies[0].wait()
    gate_part = dot(normed, weights[0], ((1,), (1,)))
    copies[1].wait()
    up_part = dot(normed, weights[1], ((1,), (1,)))
    hidden = (silu(gate_part) * up_part).astype(BF16)
    copies[2].wait()
    layer[...] = (residual.astype(F32) + gate * dot(hidden, weights[2])).astype(BF16)


def expert_call(summed, got_up, got_down, tokens, gain, w_sgate, shared):
    vmem = pl.BlockSpec(memory_space=pltpu.VMEM)
    return pl.pallas_call(
        expert_kernel,
        out_shape=(jax.ShapeDtypeStruct(tokens.shape, BF16),) * 2,
        in_specs=[vmem] * 6 + [pl.BlockSpec(memory_space=pltpu.HBM)],
        out_specs=[vmem] * 2,
        scratch_shapes=[pltpu.VMEM(shared.shape, BF16), pltpu.SemaphoreType.DMA((3,))],
        compiler_params=pltpu.CompilerParams(vmem_limit_bytes=32 * MIB),
        cost_estimate=pl.CostEstimate(flops=800_000_000, bytes_accessed=9_000_000, transcendentals=0),
        name="expert",
    )(summed, got_up, got_down, tokens, gain, w_sgate, hold(shared))


def per_device(
    tokens,
    stretch_prompt,
    last_fill,
    ln1_gain,
    w_qk,
    w_vz,
    w_ba,
    conv_qk,
    conv_value,
    decay_log,
    dt_bias,
    norm_gain,
    w_out,
    ln2_gain,
    w_sgate,
    shared_weights,
):
    width = tokens.shape[1]
    place_y = lax.axis_index("y")
    place_core = lax.axis_index("core")
    device = lax.axis_index("z") * NX + lax.axis_index("x")
    normed = norm_call(tokens, ln1_gain)

    below = turn(normed, "y", 1, NY)
    above = turn(normed, "y", -1, NY)
    beside = turn(normed, "core", 1, NC)
    flat_vz = w_vz.reshape(width, -1)
    half_vz = flat_vz.shape[1] // 2
    weight = jnp.concatenate(
        [
            w_qk.reshape(width, -1),
            flat_vz[:, :half_vz],
            jnp.pad(w_ba.reshape(width, -1), ((0, 0), (0, 128 - 2 * HEADS))),
        ],
        axis=1,
    )
    weight_z = flat_vz[:, half_vz:]

    def project(weight, *parts):
        rows = jnp.concatenate(parts, axis=0)
        return jnp.dot(rows, weight, preferred_element_type=F32).astype(BF16)

    low, high, weight = lax.optimization_barrier(
        (below[: ROWS // 2], above[ROWS // 2 :], weight)
    )
    across_up = turn(low, "y", 1, NY)
    across_down = turn(high, "y", -1, NY)
    piece_a = project(weight, normed, beside)
    above_beside = turn(above, "core", 1, NC)
    below_beside = turn(below, "core", 1, NC)
    piece_b = project(weight, above, below, above_beside, below_beside)
    across_up, across_down, piece_b = lax.optimization_barrier((across_up, across_down, piece_b))
    across = jnp.concatenate([across_up, across_down], axis=0)
    across_beside = turn(across, "core", 1, NC)
    piece_c = project(weight, across, across_beside)
    pieces = (piece_a, piece_b, piece_c)
    shared_weights, tied = lax.optimization_barrier((shared_weights, across))
    gathered = lax.all_gather(shared_weights, ("y", "core"), axis=1, tiled=True)

    first_slot = device * 2
    before = jnp.concatenate([jnp.full((1,), -1, jnp.int32), stretch_prompt])
    later = jnp.concatenate([stretch_prompt, jnp.full((1,), -1, jnp.int32)])
    current = lax.dynamic_slice_in_dim(stretch_prompt, first_slot, 2)
    starts = current != lax.dynamic_slice_in_dim(before, first_slot, 2)
    finishes = current != lax.dynamic_slice_in_dim(later, first_slot + 1, 2)
    fill = jnp.where(finishes, lax.dynamic_slice_in_dim(last_fill, first_slot, 2), STRETCH)
    scal = jnp.concatenate(
        [jnp.stack([place_y, place_core]).astype(jnp.int32), starts.astype(jnp.int32), fill]
    )

    last_place = (NY - 1 - place_y) * NC + (NC - 1 - place_core)
    ends = piece_a[ROWS - LEAD : ROWS, :COL_BA]
    for (steps, other), (piece, block) in PLACES.items():
        rows = pieces[piece][(block + 1) * ROWS - LEAD : (block + 1) * ROWS, :COL_BA]
        ends = jnp.where(last_place == steps * NC + other, rows, ends)
    tail = push(ends, ("z", "x"), 1, NZ * NX)

    def gates(*parts):
        rows = jnp.concatenate(parts, axis=0)
        gate = jnp.dot(rows, weight_z, preferred_element_type=F32).astype(BF16)
        return gate.reshape(NY, ROWS, -1)

    gates_beside = gates(beside, above_beside, across_beside, below_beside)
    gates_own = gates(normed, above, tied, below)
    tail, gates_own = lax.optimization_barrier((tail, gates_own))
    taps_qk = conv_qk.astype(F32)
    taps_kv = jnp.concatenate([taps_qk[:, 1, :], conv_value.astype(F32)], axis=1)
    pad = ((HEADS, 128 - 2 * HEADS),)
    decay = jnp.pad(decay_log, pad)[None, :]
    bias = jnp.pad(dt_bias, pad)[None, :]
    xend, xs, vs, khat, logs = state_call(scal, pieces, tail, taps_kv, decay, bias)

    parts = lax.all_to_all(xend, "x", 0, 0, tiled=True)
    parts, gates_beside = lax.optimization_barrier((parts, gates_beside))
    leads, whole, sums = row_call(parts)
    earlier = [push(whole if steps < 4 else sums, "z", steps, NZ) for steps in (1, 2, 3, 4)]
    openings = open_call(earlier, leads)
    opening = lax.all_to_all(openings, "x", 0, 0, tiled=True)

    found = read_call(scal, pieces, tail[:, :COL_K], taps_qk[:, 0, :], xs, vs, khat, logs)

    gain = norm_gain.astype(F32)[None, :]
    given = out_call(1, scal, found, gates_beside, opening, gain, w_out)
    received = turn(given, "core", 1, NC)
    own = out_call(0, scal, found, gates_own, opening, gain, w_out)

    def add(left, right):
        return (left.astype(F32) + right.astype(F32)).astype(BF16)

    summed = add(own, received)
    half = width // 2
    pass_up = turn(summed[2, :, :half], "y", 1, NY)
    pass_down = turn(summed[2, :, half:], "y", -1, NY)
    up = jnp.concatenate([add(summed[1, :, :half], pass_up), summed[1, :, half:]], axis=1)
    down = jnp.concatenate([summed[3, :, :half], add(summed[3, :, half:], pass_down)], axis=1)
    got_up = turn(up, "y", 1, NY)
    got_down = turn(down, "y", -1, NY)
    return expert_call(
        summed[0], got_up, got_down, tokens, ln2_gain, w_sgate, gathered
    )


def solution(mesh):
    fine = Mesh(mesh.devices.reshape(NZ, NX, NY, NC), ("z", "x", "y", "core"))
    rows = P(("z", "x", "y", "core"), None)
    head = ("y", "core")
    return jax.shard_map(
        per_device,
        mesh=fine,
        in_specs=(
            rows,
            P(),
            P(),
            P(),
            P(None, None, head),
            P(None, None, head),
            P(None, None, head),
            P(None, None, head),
            P(None, head),
            P(head),
            P(head),
            P(),
            P(head, None),
            P(),
            P(),
            P(None, head, None),
        ),
        out_specs=(rows, rows),
        check_vma=False,
    )
```

time: 255 us -> 170 us (0.67)
  local copies, waits for them, and re-layouts: 60.1 us -> 11.5 us
  Pallas kernels: 76.3 us -> 41.6 us
  other arithmetic: 9.24 us -> 4.12 us
  waiting for transfers between devices: 23.7 us -> 28.3 us
    pallas_call x1, Pallas kernels: 57.9 us -> 14.5 us  [state_call(): pl.pallas_call(state_kernel, out_shape=(jax.ShapeDtypeStruct((HEADS, DK,...]
    slice x6 -> x4, local copies, waits for them, and re-layouts: 17.9 us -> 1.42 us  [the longest x1 1.16 us: per_device(): below[:ROWS // 2]]
    squeeze x5 -> x2, local copies, waits for them, and re-layouts: 11.2 us -> 0.12 us  [the longest x1 0.08 us: per_device(): summed[3, :, :half]]
    concatenate x1, local copies, waits for them, and re-layouts: 10.5 us -> 0.02 us  [per_device(): across = jnp.concatenate([across_up, across_down], axis=0)]
    pallas_call x6 -> x7, Pallas kernels: 18.5 us -> 27.1 us  [the longest x2 8.02 us: out_call(): pl.pallas_call(lambda *refs: out_kernel(other, *refs), grid=(NY // 2,), o...]
    ppermute x12 -> x13, waiting for transfers between devices: 17.1 us -> 25.3 us  [turn(): lax.ppermute(value, axis, [(i, (i + steps) % count) for i in range(count)])]
    unnamed x84 -> x62, local copies, waits for them, and re-layouts: 16.5 us -> 9.84 us
    all_to_all x1, waiting for transfers between devices: 4.8 us -> 1.68 us  [per_device(): parts = lax.all_to_all(xend, 'x', 0, 0, tiled=True)]
  transfers between devices with their start and end apart: 19 -> 21, of which waited for: 7 -> 9; matrix products, arithmetic and copies ran while one was open for 25% -> 19% of each run, Pallas kernels for 30% -> 21%
where the time goes in v2:
time: 170 us; the launch traced here: 167 us
  starting transfers between devices  46.6 us (27%)
  Pallas kernels  41.6 us (24%)
  waiting for transfers between devices  28.3 us (17%)
  matrix products  20.7 us (12%)
  between operations  14.6 us (9%)
  local copies, waits for them, and re-layouts  11.5 us (7%)
  other arithmetic  4.12 us (2%)
    ppermute x13, waiting for transfers between devices, turn(): lax.ppermute(value, axis, [(i, (i + steps) % count) for i in range(count)])  25.3 us
    ppermute x13, starting transfers between devices, turn(): lax.ppermute(value, axis, [(i, (i + steps) % count) for i in range(count)])  20.4 us
    ppermute x5, starting transfers between devices, push(): lax.ppermute(value, axis, [(i, i + steps) for i in range(count - steps)])  18.8 us
    pallas_call x1, Pallas kernels, state_call(): pl.pallas_call(state_kernel, out_shape=(jax.ShapeDtypeStruct((HEADS, DK,...  14.5 us
    dot_general x3, matrix products, project(): return jnp.dot(rows, weight, preferred_element_type=F32).astype(BF16)  13.7 us
    unnamed x62, local copies, waits for them, and re-layouts  9.84 us
    pallas_call x2, Pallas kernels, out_call(): pl.pallas_call(lambda *refs: out_kernel(other, *refs), grid=(NY // 2,), o...  8.02 us
    pallas_call x1, Pallas kernels, read_call(): pl.pallas_call(read_kernel, out_shape=pltpu.HBM((NC, NY, HEADS, ROWS, 2 *...  7.81 us
  transfers between devices with their start and end apart: 21, of which 9 were waited for; matrix products, arithmetic and copies ran while one was open for 19% of the time, Pallas kernels for 21%

profile of v2, /device:TPU:1, one launch (start us, length us, event | category | flops | bytes accessed | tf_op | source)
XLA Modules:
  0.0 167.4 jit_solution(5516817472928246855)
XLA Ops:
  9.3 3.6 %collective-permute-start.2 = (bf16[128,2048]{1,0:T(8,128)(2,1)}, bf16[128,2048]{1,0:T(8,128)(2,1)S(1)}, u32[]{:S(2)}, u32[]{:S(2)}) collective-permute-start(bf16[128,2048]{1,0:T(8,128)(2,1)} %norm.1), channel_id=1, source_target_pairs={{0,6},{2,0},{4,2},{6,4},{1,7},{3,1},{5,3},{7,5},{8,14},{10,8},{12,... | collective-permute-start | bytes 1572872 | tf_op jit(solution)/shard_map/ppermute | solution.py:62
  12.8 3.4 %copy.22 = bf16[256,8,2,512]{3,1,2,0:T(8,128)(2,1)S(1)} copy(bf16[256,8,2,512]{3,2,1,0:T(2,128)(2,1)} %bitcast.48) | data formatting | bytes 8388608
  31.8 2.7 %collective-permute-start.4 = (bf16[64,2048]{1,0:T(8,128)(2,1)S(1)}, bf16[64,2048]{1,0:T(8,128)(2,1)S(1)}, u32[]{:S(2)}, u32[]{:S(2)}) collective-permute-start(bf16[64,2048]{1,0:T(8,128)(2,1)S(1)} %slice.90), channel_id=1, source_target_pairs={{0,6},{2,0},{4,2},{6,4},{1,7},{3,1},{5,3},{7,5},{8,14},{10,8},{12,... | collective-permute-start | bytes 786440 | tf_op jit(solution)/shard_map/ppermute | solution.py:62
  34.5 5.3 %convolution_convert_fusion.piece_b = bf16[512,1152]{1,0:T(8,128)(2,1)} fusion(bf16[2048,1152]{1,0:T(8,128)(2,1)S(1)} %fusion.1, bf16[128,2048]{1,0:T(8,128)(2,1)S(1)} %collective-permute-done.6, bf16[128,2048]{1,0:T(8,128)(2,1)S(1)} %collective-permute-done.5, bf16[128,2048]{1,0:T(8,128)(2,1)} %collective-permute-done.1, ...), kind=kOutput, calls=%fused_computation.4 | convolution fusion | flops 2424897536 | bytes 7995392 | tf_op jit(solution)/shard_map/dot_general | solution.py:594
  43.6 4.0 %convolution_convert_fusion.2.piece_a = bf16[256,1152]{1,0:T(8,128)(2,1)S(1)} fusion(bf16[2048,1152]{1,0:T(8,128)(2,1)} %copy-done.5, bf16[128,2048]{1,0:T(8,128)(2,1)} %collective-permute-done, bf16[128,2048]{1,0:T(8,128)(2,1)S(1)} %copy-done.7), kind=kOutput, calls=%fused_computation.8 | convolution fusion | flops 1210351616 | bytes 6356992 | tf_op jit(solution)/shard_map/dot_general | solution.py:594
  47.7 4.3 %convolution_convert_fusion.1.piece_c = bf16[256,1152]{1,0:T(8,128)(2,1)S(1)} fusion(bf16[2048,1152]{1,0:T(8,128)(2,1)} %copy-done.5, bf16[128,2048]{1,0:T(8,128)(2,1)S(1)} %collective-permute-done.7, bf16[64,2048]{1,0:T(8,128)(2,1)S(1)} %collective-permute-done.4, bf16[64,2048]{1,0:T(8,128)(2,1)S(1)} %collective-permute-done.3), kind=kOutput, calls=%fused_computation.7 | convolution fusion | flops 1211400192 | bytes 6356992 | tf_op jit(solution)/shard_map/dot_general | solution.py:594
  53.0 3.3 %collective-permute-start.8 = (bf16[16,1024]{1,0:T(8,128)(2,1)S(1)}, bf16[16,1024]{1,0:T(8,128)(2,1)S(1)}, u32[]{:S(2)}, u32[]{:S(2)}) collective-permute-start(bf16[16,1024]{1,0:T(8,128)(2,1)S(1)} %fusion.46), channel_id=1, source_target_pairs={{0,8},{8,16},{16,24},{24,32},{32,40},{40,48},{48,56},{56,64},{64,7... | collective-permute-start | bytes 98312 | tf_op jit(solution)/shard_map/ppermute | solution.py:66
  56.3 3.2 %fusion.23 = bf16[512,512]{1,0:T(8,128)(2,1)} fusion(bf16[2048,1024]{1,0:T(8,128)(2,1)S(1)} %bitcast.46, bf16[128,2048]{1,0:T(8,128)(2,1)} %collective-permute-done.1, bf16[128,2048]{1,0:T(8,128)(2,1)S(1)} %constant_dynamic-update-slice_fusion, bf16[128,2048]{1,0:T(8,128)(2,1)S(1)} %collective-permute-done.2, bf16[128,2048]{1,0:T(8,128)(2,1)S(1)} %copy-done.7), kind=kOutput, calls=%fused_computation.30 | convolution fusion | flops 1082392576 | bytes 4718592 | tf_op jit(solution)/shard_map/dot_general | solution.py:633
  59.5 14.5 %state.1 = (bf16[4,128,256]{2,1,0:T(8,128)(2,1)}, bf16[8,2,128,512]{3,2,1,0:T(8,128)(2,1)}, bf16[8,4,128,256]{3,2,1,0:T(8,128)(2,1)}, bf16[8,2,128,128]{3,2,1,0:T(8,128)(2,1)}, f32[8,128,128]{2,1,0:T(8,128)}) custom-call(s32[6]{0:T(128)S(1)} %pad_add_fusion.2.scal.refs_0_, bf16[256,1152]{1,0:T(8,128)(2,1)} %copy-done.14, ...), custom_call_target="tpu_custom_call" | custom-call | flops 6000000000 | bytes 20000000 | tf_op jit(solution)/shard_map/state/pallas_call | solution.py:295
  74.0 4.1 %all-to-all-start = ((bf16[4,128,256]{2,1,0:T(8,128)(2,1)}), bf16[4,128,256]{2,1,0:T(8,128)(2,1)S(1)}, u32[]{:S(2)}, u32[]{:S(2)}) async-start(bf16[4,128,256]{2,1,0:T(8,128)(2,1)} %get-tuple-element.35), calls=%async_computation | async-start | bytes 524288 | tf_op jit(solution)/shard_map/all_to_all | solution.py:646
  78.1 3.9 %fusion.28 = bf16[512,512]{1,0:T(8,128)(2,1)} fusion(bf16[2048,1024]{1,0:T(8,128)(2,1)} %bitcast.45, bf16[128,2048]{1,0:T(8,128)(2,1)S(1)} %copy-done.25, bf16[128,2048]{1,0:T(8,128)(2,1)S(1)} %copy-done.27, bf16[128,2048]{1,0:T(8,128)(2,1)S(1)} %copy-done.23, bf16[128,2048]{1,0:T(8,128)(2,1)} %collective-permute-done), kind=kOutput, calls=%fused_computation.31 | convolution fusion | flops 1082392576 | bytes 4718592 | tf_op jit(solution)/shard_map/dot_general | solution.py:633
  86.4 5.0 %collective-permute-start.10 = (bf16[128,256]{1,0:T(8,128)(2,1)}, bf16[128,256]{1,0:T(8,128)(2,1)S(1)}, u32[]{:S(2)}, u32[]{:S(2)}) collective-permute-start(bf16[128,256]{1,0:T(8,128)(2,1)} %get-tuple-element.37), channel_id=1, source_target_pairs={{0,64},{32,96},{64,128},{96,160},{128,192},{160,224},{1,65},{33,97... | collective-permute-start | bytes 196616 | tf_op jit(solution)/shard_map/ppermute | solution.py:66
  91.4 6.2 %collective-permute-start.11 = (bf16[128,256]{1,0:T(8,128)(2,1)}, bf16[128,256]{1,0:T(8,128)(2,1)S(1)}, u32[]{:S(2)}, u32[]{:S(2)}) collective-permute-start(bf16[128,256]{1,0:T(8,128)(2,1)} %get-tuple-element.37), channel_id=1, source_target_pairs={{0,96},{32,128},{64,160},{96,192},{128,224},{1,97},{33,129},{65,16... | collective-permute-start | bytes 196616 | tf_op jit(solution)/shard_map/ppermute | solution.py:66
  97.5 2.7 %collective-permute-start.9 = (bf16[128,256]{1,0:T(8,128)(2,1)}, bf16[128,256]{1,0:T(8,128)(2,1)S(1)}, u32[]{:S(2)}, u32[]{:S(2)}) collective-permute-start(bf16[128,256]{1,0:T(8,128)(2,1)} %get-tuple-element.37), channel_id=1, source_target_pairs={{0,32},{32,64},{64,96},{96,128},{128,160},{160,192},{192,224},{1,3... | collective-permute-start | bytes 196616 | tf_op jit(solution)/shard_map/ppermute | solution.py:66
  106.3 3.3 %all-to-all-start.1 = ((bf16[4,128,128]{2,1,0:T(8,128)(2,1)}), bf16[4,128,128]{2,1,0:T(8,128)(2,1)S(1)}, u32[]{:S(2)}, u32[]{:S(2)}) async-start(bf16[4,128,128]{2,1,0:T(8,128)(2,1)} %open.1), calls=%async_computation.1 | async-start | bytes 262144 | tf_op jit(solution)/shard_map/all_to_all | solution.py:651
  109.6 7.8 %read.1.refs_1_ = bf16[2,4,4,128,256]{4,3,2,1,0:T(8,128)(2,1)} custom-call(s32[6]{0:T(128)S(1)} %pad_add_fusion.2.scal.refs_0_, bf16[256,1152]{1,0:T(8,128)(2,1)} %copy-done.14, bf16[512,1152]{1,0:T(8,128)(2,1)} %convolution_convert_fusion.piece_b, bf16[256,1152]{1,0:T(8,128)(2,1)} %copy-done.15, bf16[16,256]{1,0:T(8,128)(2,1)S(1)} %slice.79.tail, ...), custom_call_target="tpu_custom_call" | custom-call | flops 3000000000 | bytes 20000000 | tf_op jit(solution)/shard_map/read/pallas_call | solution.py:367
  117.4 4.0 %out.3 = bf16[4,128,2048]{2,1,0:T(8,128)(2,1)S(1)} custom-call(s32[6]{0:T(128)S(1)} %pad_add_fusion.2.scal.refs_0_, bf16[2,4,4,128,256]{4,3,2,1,0:T(8,128)(2,1)} %read.1.refs_1_, bf16[4,128,512]{2,1,0:T(8,128)(2,1)} %bitcast.51, bf16[4,128,128]{2,1,0:T(8,128)(2,1)S(1)} %all-to-all-done.1.refs_3_, f32[1,128]{1,0:T(1,128)S(1)} %bitcast_convert_fusion.refs_4_, ...), custom_call_target="tpu_custom_call" | custom-call | flops 1200000000 | bytes 6000000 | tf_op jit(solution)/shard_map/out/pallas_call | solution.py:498
  121.4 4.1 %collective-permute-start.13 = (bf16[4,128,2048]{2,1,0:T(8,128)(2,1)S(1)}, bf16[4,128,2048]{2,1,0:T(8,128)(2,1)S(1)}, u32[]{:S(2)}, u32[]{:S(2)}) collective-permute-start(bf16[4,128,2048]{2,1,0:T(8,128)(2,1)S(1)} %out.3), channel_id=1, source_target_pairs={{0,1},{1,0},{2,3},{3,2},{4,5},{5,4},{6,7},{7,6},{8,9},{9,8},{10,11... | collective-permute-start | bytes 6291464 | tf_op jit(solution)/shard_map/ppermute | solution.py:62
  125.5 4.0 %out.2 = bf16[4,128,2048]{2,1,0:T(8,128)(2,1)S(1)} custom-call(s32[6]{0:T(128)S(1)} %pad_add_fusion.2.scal.refs_0_, bf16[2,4,4,128,256]{4,3,2,1,0:T(8,128)(2,1)} %read.1.refs_1_, bf16[4,128,512]{2,1,0:T(8,128)(2,1)} %bitcast.50, bf16[4,128,128]{2,1,0:T(8,128)(2,1)S(1)} %all-to-all-done.1.refs_3_, f32[1,128]{1,0:T(1,128)S(1)} %bitcast_convert_fusion.refs_4_, ...), custom_call_target="tpu_custom_call" | custom-call | flops 1200000000 | bytes 6000000 | tf_op jit(solution)/shard_map/out/pallas_call | solution.py:498
  130.6 2.7 %collective-permute-start.16 = (bf16[128,1024]{1,0:T(8,128)(2,1)S(1)}, bf16[128,1024]{1,0:T(8,128)(2,1)S(1)}, u32[]{:S(2)}, u32[]{:S(2)}) collective-permute-start(bf16[128,1024]{1,0:T(8,128)(2,1)S(1)} %get-tuple-element.43), channel_id=1, source_target_pairs={{0,6},{2,0},{4,2},{6,4},{1,7},{3,1},{5,3},{7,5},{8,14},{10,8},{12,... | collective-permute-start | bytes 786440 | tf_op jit(solution)/shard_map/ppermute | solution.py:62
  133.3 6.2 %collective-permute-done.14 = bf16[128,1024]{1,0:T(8,128)(2,1)S(1)} collective-permute-done((bf16[128,1024]{1,0:T(8,128)(2,1)S(1)}, bf16[128,1024]{1,0:T(8,128)(2,1)S(1)}, u32[]{:S(2)}, u32[]{:S(2)}) %collective-permute-start.14) | collective-permute-done | bytes 262176 | tf_op jit(solution)/shard_map/ppermute | solution.py:62
  142.5 9.9 %collective-permute-done.17.got_down = bf16[128,2048]{1,0:T(8,128)(2,1)S(1)} collective-permute-done((bf16[128,2048]{1,0:T(8,128)(2,1)S(1)}, bf16[128,2048]{1,0:T(8,128)(2,1)S(1)}, u32[]{:S(2)}, u32[]{:S(2)}) %collective-permute-start.17) | collective-permute-done | bytes 524320 | tf_op jit(solution)/shard_map/ppermute | solution.py:62
  152.4 3.2 %collective-permute-done.15.got_up = bf16[128,2048]{1,0:T(8,128)(2,1)S(1)} collective-permute-done((bf16[128,2048]{1,0:T(8,128)(2,1)S(1)}, bf16[128,2048]{1,0:T(8,128)(2,1)S(1)}, u32[]{:S(2)}, u32[]{:S(2)}) %collective-permute-start.15) | collective-permute-done | bytes 524320 | tf_op jit(solution)/shard_map/ppermute | solution.py:62
  155.7 4.9 %expert.1 = (bf16[128,2048]{1,0:T(8,128)(2,1)}, bf16[128,2048]{1,0:T(8,128)(2,1)}) custom-call(bf16[128,2048]{1,0:T(8,128)(2,1)S(1)} %slice_bitcast_fusion.summed, bf16[128,2048]{1,0:T(8,128)(2,1)S(1)} %collective-permute-done.15.got_up, bf16[128,2048]{1,0:T(8,128)(2,1)S(1)} %collective-permute-done.17.got_down, bf16[128,2048]{1,0:T(8,128)(2,1)S(1)} %copy-done, ...), custom_call_target="tpu_custom_call" | custom-call | flops 800000000 | bytes 9000000 | tf_op jit(solution)/shard_map/expert/pallas_call | solution.py:541
  (118 shorter events, 36.8 us)
Async XLA Ops:
  7.2 148.5 %all-gather.2.cloned.1.call-start = ((), (), s32[]{:S(2)}) async-start(), calls=%async_computation.2 | async-start | bytes 7077888 | tf_op jit(solution)/shard_map/all_gather | solution.py:611
  9.3 14.5 %collective-permute-start.2 = (bf16[128,2048]{1,0:T(8,128)(2,1)}, bf16[128,2048]{1,0:T(8,128)(2,1)S(1)}, u32[]{:S(2)}, u32[]{:S(2)}) collective-permute-start(bf16[128,2048]{1,0:T(8,128)(2,1)} %norm.1), channel_id=1, source_target_pairs={{0,6},{2,0},{4,2},{6,4},{1,7},{3,1},{5,3},{7,5},{8,14},{10,8},{12,... | collective-permute-start | bytes 1572872 | tf_op jit(solution)/shard_map/ppermute | solution.py:62
  12.8 14.0 %collective-permute-start.1 = (bf16[128,2048]{1,0:T(8,128)(2,1)}, bf16[128,2048]{1,0:T(8,128)(2,1)}, u32[]{:S(2)}, u32[]{:S(2)}) collective-permute-start(bf16[128,2048]{1,0:T(8,128)(2,1)} %norm.1), channel_id=1, source_target_pairs={{0,2},{2,4},{4,6},{6,0},{1,3},{3,5},{5,7},{7,1},{8,10},{10,12},{12... | collective-permute-start | bytes 1572872 | tf_op jit(solution)/shard_map/ppermute | solution.py:62
  23.8 10.7 %collective-permute-start.5 = (bf16[128,2048]{1,0:T(8,128)(2,1)S(1)}, bf16[128,2048]{1,0:T(8,128)(2,1)S(1)}, u32[]{:S(2)}, u32[]{:S(2)}) collective-permute-start(bf16[128,2048]{1,0:T(8,128)(2,1)S(1)} %collective-permute-done.2), channel_id=1, source_target_pairs={{0,1},{1,0},{2,3},{3,2},{4,5},{5,4},{6,7},{7,6},{8,9},{9,8},{10,11... | collective-permute-start | bytes 1572872 | tf_op jit(solution)/shard_map/ppermute | solution.py:62
  26.8 7.7 %collective-permute-start.6 = (bf16[128,2048]{1,0:T(8,128)(2,1)}, bf16[128,2048]{1,0:T(8,128)(2,1)S(1)}, u32[]{:S(2)}, u32[]{:S(2)}) collective-permute-start(bf16[128,2048]{1,0:T(8,128)(2,1)} %collective-permute-done.1), channel_id=1, source_target_pairs={{0,1},{1,0},{2,3},{3,2},{4,5},{5,4},{6,7},{7,6},{8,9},{9,8},{10,11... | collective-permute-start | bytes 1572872 | tf_op jit(solution)/shard_map/ppermute | solution.py:62
  31.7 9.2 %collective-permute-start.3 = (bf16[64,2048]{1,0:T(8,128)(2,1)S(1)}, bf16[64,2048]{1,0:T(8,128)(2,1)S(1)}, u32[]{:S(2)}, u32[]{:S(2)}) collective-permute-start(bf16[64,2048]{1,0:T(8,128)(2,1)S(1)} %slice.89), channel_id=1, source_target_pairs={{0,2},{2,4},{4,6},{6,0},{1,3},{3,5},{5,7},{7,1},{8,10},{10,12},{12... | collective-permute-start | bytes 786440 | tf_op jit(solution)/shard_map/ppermute | solution.py:62
  31.8 9.1 %collective-permute-start.4 = (bf16[64,2048]{1,0:T(8,128)(2,1)S(1)}, bf16[64,2048]{1,0:T(8,128)(2,1)S(1)}, u32[]{:S(2)}, u32[]{:S(2)}) collective-permute-start(bf16[64,2048]{1,0:T(8,128)(2,1)S(1)} %slice.90), channel_id=1, source_target_pairs={{0,6},{2,0},{4,2},{6,4},{1,7},{3,1},{5,3},{7,5},{8,14},{10,8},{12,... | collective-permute-start | bytes 786440 | tf_op jit(solution)/shard_map/ppermute | solution.py:62
  41.1 2.5 %collective-permute-start = (bf16[128,2048]{1,0:T(8,128)(2,1)S(1)}, bf16[128,2048]{1,0:T(8,128)(2,1)}, u32[]{:S(2)}, u32[]{:S(2)}) collective-permute-start(bf16[128,2048]{1,0:T(8,128)(2,1)S(1)} %copy-done.7), channel_id=1, source_target_pairs={{0,1},{1,0},{2,3},{3,2},{4,5},{5,4},{6,7},{7,6},{8,9},{9,8},{10,11... | collective-permute-start | bytes 1572872 | tf_op jit(solution)/shard_map/ppermute | solution.py:62
  42.3 5.4 %collective-permute-start.7 = (bf16[128,2048]{1,0:T(8,128)(2,1)S(1)}, bf16[128,2048]{1,0:T(8,128)(2,1)S(1)}, u32[]{:S(2)}, u32[]{:S(2)}) collective-permute-start(bf16[128,2048]{1,0:T(8,128)(2,1)S(1)} %constant_dynamic-update-slice_fusion), channel_id=1, source_target_pairs={{0,1},{1,0},{2,3},{3,2},{4,5},{5,4},{6,7},{7,6},{8,9},{9,8},{10,11... | collective-permute-start | bytes 1572872 | tf_op jit(solution)/shard_map/ppermute | solution.py:62
  53.0 6.5 %collective-permute-start.8 = (bf16[16,1024]{1,0:T(8,128)(2,1)S(1)}, bf16[16,1024]{1,0:T(8,128)(2,1)S(1)}, u32[]{:S(2)}, u32[]{:S(2)}) collective-permute-start(bf16[16,1024]{1,0:T(8,128)(2,1)S(1)} %fusion.46), channel_id=1, source_target_pairs={{0,8},{8,16},{16,24},{24,32},{32,40},{40,48},{48,56},{56,64},{64,7... | collective-permute-start | bytes 98312 | tf_op jit(solution)/shard_map/ppermute | solution.py:66
  74.0 9.7 %all-to-all-start = ((bf16[4,128,256]{2,1,0:T(8,128)(2,1)}), bf16[4,128,256]{2,1,0:T(8,128)(2,1)S(1)}, u32[]{:S(2)}, u32[]{:S(2)}) async-start(bf16[4,128,256]{2,1,0:T(8,128)(2,1)} %get-tuple-element.35), calls=%async_computation | async-start | bytes 524288 | tf_op jit(solution)/shard_map/all_to_all | solution.py:646
  86.4 16.9 %collective-permute-start.10 = (bf16[128,256]{1,0:T(8,128)(2,1)}, bf16[128,256]{1,0:T(8,128)(2,1)S(1)}, u32[]{:S(2)}, u32[]{:S(2)}) collective-permute-start(bf16[128,256]{1,0:T(8,128)(2,1)} %get-tuple-element.37), channel_id=1, source_target_pairs={{0,64},{32,96},{64,128},{96,160},{128,192},{160,224},{1,65},{33,97... | collective-permute-start | bytes 196616 | tf_op jit(solution)/shard_map/ppermute | solution.py:66
  91.4 11.9 %collective-permute-start.11 = (bf16[128,256]{1,0:T(8,128)(2,1)}, bf16[128,256]{1,0:T(8,128)(2,1)S(1)}, u32[]{:S(2)}, u32[]{:S(2)}) collective-permute-start(bf16[128,256]{1,0:T(8,128)(2,1)} %get-tuple-element.37), channel_id=1, source_target_pairs={{0,96},{32,128},{64,160},{96,192},{128,224},{1,97},{33,129},{65,16... | collective-permute-start | bytes 196616 | tf_op jit(solution)/shard_map/ppermute | solution.py:66
  97.5 5.8 %collective-permute-start.9 = (bf16[128,256]{1,0:T(8,128)(2,1)}, bf16[128,256]{1,0:T(8,128)(2,1)S(1)}, u32[]{:S(2)}, u32[]{:S(2)}) collective-permute-start(bf16[128,256]{1,0:T(8,128)(2,1)} %get-tuple-element.37), channel_id=1, source_target_pairs={{0,32},{32,64},{64,96},{96,128},{128,160},{160,192},{192,224},{1,3... | collective-permute-start | bytes 196616 | tf_op jit(solution)/shard_map/ppermute | solution.py:66
  100.2 3.0 %collective-permute-start.12 = (bf16[128,128]{1,0:T(8,128)(2,1)}, bf16[128,128]{1,0:T(8,128)(2,1)S(1)}, u32[]{:S(2)}, u32[]{:S(2)}) collective-permute-start(bf16[128,128]{1,0:T(8,128)(2,1)} %get-tuple-element.38), channel_id=1, source_target_pairs={{0,128},{32,160},{64,192},{96,224},{1,129},{33,161},{65,193},{97,2... | collective-permute-start | bytes 98312 | tf_op jit(solution)/shard_map/ppermute | solution.py:66
  106.3 11.2 %all-to-all-start.1 = ((bf16[4,128,128]{2,1,0:T(8,128)(2,1)}), bf16[4,128,128]{2,1,0:T(8,128)(2,1)S(1)}, u32[]{:S(2)}, u32[]{:S(2)}) async-start(bf16[4,128,128]{2,1,0:T(8,128)(2,1)} %open.1), calls=%async_computation.1 | async-start | bytes 262144 | tf_op jit(solution)/shard_map/all_to_all | solution.py:651
  121.4 8.1 %collective-permute-start.13 = (bf16[4,128,2048]{2,1,0:T(8,128)(2,1)S(1)}, bf16[4,128,2048]{2,1,0:T(8,128)(2,1)S(1)}, u32[]{:S(2)}, u32[]{:S(2)}) collective-permute-start(bf16[4,128,2048]{2,1,0:T(8,128)(2,1)S(1)} %out.3), channel_id=1, source_target_pairs={{0,1},{1,0},{2,3},{3,2},{4,5},{5,4},{6,7},{7,6},{8,9},{9,8},{10,11... | collective-permute-start | bytes 6291464 | tf_op jit(solution)/shard_map/ppermute | solution.py:62
  130.4 9.0 %collective-permute-start.14 = (bf16[128,1024]{1,0:T(8,128)(2,1)S(1)}, bf16[128,1024]{1,0:T(8,128)(2,1)S(1)}, u32[]{:S(2)}, u32[]{:S(2)}) collective-permute-start(bf16[128,1024]{1,0:T(8,128)(2,1)S(1)} %get-tuple-element.45), channel_id=1, source_target_pairs={{0,2},{2,4},{4,6},{6,0},{1,3},{3,5},{5,7},{7,1},{8,10},{10,12},{12... | collective-permute-start | bytes 786440 | tf_op jit(solution)/shard_map/ppermute | solution.py:62
  130.5 25.2 %copy-start = (bf16[128,2048]{1,0:T(8,128)(2,1)S(1)}, bf16[128,2048]{1,0:T(8,128)(2,1)}, u32[]{:S(2)}) copy-start(bf16[128,2048]{1,0:T(8,128)(2,1)} %tokens.3) | copy-start | bytes 1572868
  130.5 25.2 %copy-start.1 = (bf16[2048]{0:T(1024)(128)(2,1)S(1)}, bf16[2048]{0:T(1024)(128)(2,1)}, u32[]{:S(2)}) copy-start(bf16[2048]{0:T(1024)(128)(2,1)} %gain.3) | copy-start | bytes 12292
  130.5 25.1 %copy-start.2 = (bf16[2048]{0:T(1024)(128)(2,1)S(1)}, bf16[2048]{0:T(1024)(128)(2,1)}, u32[]{:S(2)}) copy-start(bf16[2048]{0:T(1024)(128)(2,1)} %w_sgate.1) | copy-start | bytes 12292
  130.6 8.9 %collective-permute-start.16 = (bf16[128,1024]{1,0:T(8,128)(2,1)S(1)}, bf16[128,1024]{1,0:T(8,128)(2,1)S(1)}, u32[]{:S(2)}, u32[]{:S(2)}) collective-permute-start(bf16[128,1024]{1,0:T(8,128)(2,1)S(1)} %get-tuple-element.43), channel_id=1, source_target_pairs={{0,6},{2,0},{4,2},{6,4},{1,7},{3,1},{5,3},{7,5},{8,14},{10,8},{12,... | collective-permute-start | bytes 786440 | tf_op jit(solution)/shard_map/ppermute | solution.py:62
  139.7 12.7 %collective-permute-start.17 = (bf16[128,2048]{1,0:T(8,128)(2,1)S(1)}, bf16[128,2048]{1,0:T(8,128)(2,1)S(1)}, u32[]{:S(2)}, u32[]{:S(2)}) collective-permute-start(bf16[128,2048]{1,0:T(8,128)(2,1)S(1)} %pad_maximum_fusion.7), channel_id=1, source_target_pairs={{0,6},{2,0},{4,2},{6,4},{1,7},{3,1},{5,3},{7,5},{8,14},{10,8},{12,... | collective-permute-start | bytes 1572872 | tf_op jit(solution)/shard_map/ppermute | solution.py:62
  142.4 13.3 %collective-permute-start.15 = (bf16[128,2048]{1,0:T(8,128)(2,1)S(1)}, bf16[128,2048]{1,0:T(8,128)(2,1)S(1)}, u32[]{:S(2)}, u32[]{:S(2)}) collective-permute-start(bf16[128,2048]{1,0:T(8,128)(2,1)S(1)} %pad_maximum_fusion.6), channel_id=1, source_target_pairs={{0,2},{2,4},{4,6},{6,0},{1,3},{3,5},{5,7},{7,1},{8,10},{10,12},{12... | collective-permute-start | bytes 1572872 | tf_op jit(solution)/shard_map/ppermute | solution.py:62
  (26 other events, 207.2 us)
Sparse Core Ops, SparseCore 0:
  41.2 46.7 all-gather.1
